TPU v7x, 256 devices: a whole 4x4x8 slice. The times are simulated.
256 devices in a mesh: frame: 8 (over z_hi, core), tile: 32 (over z_lo, y, x).
Axes of the slice: x: 4, y: 4, z: 8 (z_hi: 4, z_lo: 2; z = z_hi * 2 + z_lo), core: 2. Of those that a mesh axis runs over, the one named last changes fastest.
Arguments:
- queries: bfloat16 [32768, 4096], P(('frame', 'tile')), may hold values from -100 to 100
- keys: bfloat16 [32768, 4096], P(('frame', 'tile')), may hold values from -6 to 6
- values: bfloat16 [32768, 4096], P(('frame', 'tile')), may hold values from -6 to 6
- out_grad: bfloat16 [32768, 4096], P(('frame', 'tile')), may hold values from -6 to 6
- key_lists: int32 [256, 6], P('frame'), may hold values from 0 to 95, as said below
- key_counts: int32 [256], P('frame'), may hold values from 2 to 6
Outputs:
- query_grad: bfloat16 [32768, 4096], P(('frame', 'tile'))
- key_grad: bfloat16 [32768, 4096], P(('frame', 'tile'))
- value_grad: bfloat16 [32768, 4096], P(('frame', 'tile'))
Inputs may be any that keep to these rules, and one draw needn't show every extreme that they name: `key_lists`: each row holds distinct window positions; its first entry is the query's own block, and no entry names a block outside the clip. All entries of the rows of one frame group together name at most 16 distinct blocks of the previous group and at most 16 of the next.
All inputs are finite; a program needn't handle non-finite values.
Results may differ from a plain program's by a relative error of at most 0.0052.
Values may be sent and summed in bfloat16 or wider, within the bound.
A program may use at most 128 MiB of HBM per device.

v0:
```python
import jax
import jax.numpy as jnp
from jax import lax
from jax.sharding import PartitionSpec as P

HEAD_DIM = 128
BLOCK = 128


def shifted(array, axis, by):
    size = lax.axis_size(axis)
    pairs = [(i, i + by) for i in range(size) if 0 <= i + by < size]
    return lax.ppermute(array, axis, pairs)


def attend_back(q_blocks, g_blocks, k_all, v_all, lists, valid, scale):
    k_listed = jnp.take(k_all, lists, axis=0)
    v_listed = jnp.take(v_all, lists, axis=0)
    allowed = valid[:, None, None, :, None]
    score = (
        jnp.einsum("nahd,nsbhd->nhasb", q_blocks, k_listed, preferred_element_type=jnp.float32)
        * scale
    )
    masked = jnp.where(allowed, score, -1e30)
    top = jnp.max(masked, axis=(3, 4))
    total = jnp.sum(jnp.exp(masked - top[..., None, None]), axis=(3, 4))
    lse = top + jnp.log(total)
    prob = jnp.where(allowed, jnp.exp(score - lse[..., None, None]), 0.0)
    plow = prob.astype(jnp.bfloat16)
    attn_out = jnp.einsum("nhasb,nsbhd->nahd", plow, v_listed, preferred_element_type=jnp.float32)
    delta = jnp.sum(g_blocks.astype(jnp.float32) * attn_out, axis=3).transpose(0, 2, 1)
    dprob = jnp.einsum("nahd,nsbhd->nhasb", g_blocks, v_listed, preferred_element_type=jnp.float32)
    dscore = (prob * (dprob - delta[..., None, None])).astype(jnp.bfloat16)
    dq = jnp.einsum("nhasb,nsbhd->nahd", dscore, k_listed, preferred_element_type=jnp.float32)
    key_terms = jnp.einsum(
        "nhasb,nahd->nsbhd", dscore, q_blocks, preferred_element_type=jnp.float32
    )
    value_terms = jnp.einsum(
        "nhasb,nahd->nsbhd", plow, g_blocks, preferred_element_type=jnp.float32
    )
    dk = jnp.zeros(k_all.shape, jnp.float32).at[lists].add(key_terms)
    dv = jnp.zeros(k_all.shape, jnp.float32).at[lists].add(value_terms)
    return (dq * scale, dk * scale, dv)


def local(queries, keys, values, out_grad, key_lists, key_counts):
    scale = HEAD_DIM ** (-0.5)
    q_rows, k_rows, v_rows, g_rows = (
        lax.all_to_all(queries, "tile", split_axis=1, concat_axis=0, tiled=True),
        lax.all_to_all(keys, "tile", split_axis=1, concat_axis=0, tiled=True),
        lax.all_to_all(values, "tile", split_axis=1, concat_axis=0, tiled=True),
        lax.all_to_all(out_grad, "tile", split_axis=1, concat_axis=0, tiled=True),
    )
    frame_rows = q_rows.shape[0]
    nblk = frame_rows // BLOCK
    heads_here = q_rows.shape[1] // HEAD_DIM

    def blocks(x):
        return x.reshape(nblk, BLOCK, heads_here, HEAD_DIM)

    valid = jnp.arange(key_lists.shape[1])[None, :] < key_counts[:, None]
    k_blocks = blocks(k_rows)
    v_blocks = blocks(v_rows)
    k_before, v_before = shifted((k_blocks, v_blocks), "frame", 1)
    k_after, v_after = shifted((k_blocks, v_blocks), "frame", -1)
    k_all = jnp.concatenate([k_before, k_blocks, k_after], 0)
    v_all = jnp.concatenate([v_before, v_blocks, v_after], 0)
    dq, dk, dv = attend_back(blocks(q_rows), blocks(g_rows), k_all, v_all, key_lists, valid, scale)
    from_later_k, from_later_v = shifted(
        (dk[:nblk].astype(jnp.bfloat16), dv[:nblk].astype(jnp.bfloat16)), "frame", -1
    )
    from_prior_k, from_prior_v = shifted(
        (dk[2 * nblk :].astype(jnp.bfloat16), dv[2 * nblk :].astype(jnp.bfloat16)), "frame", 1
    )
    key_total = (
        dk[nblk : 2 * nblk] + from_later_k.astype(jnp.float32) + from_prior_k.astype(jnp.float32)
    )
    value_total = (
        dv[nblk : 2 * nblk] + from_later_v.astype(jnp.float32) + from_prior_v.astype(jnp.float32)
    )

    def flat(x):
        return x.astype(jnp.bfloat16).reshape(frame_rows, heads_here * HEAD_DIM)

    return (
        lax.all_to_all(flat(dq), "tile", split_axis=0, concat_axis=1, tiled=True),
        lax.all_to_all(flat(key_total), "tile", split_axis=0, concat_axis=1, tiled=True),
        lax.all_to_all(flat(value_total), "tile", split_axis=0, concat_axis=1, tiled=True),
    )


def solution(mesh):
    return jax.shard_map(
        local,
        mesh=mesh,
        in_specs=(
            P(("frame", "tile"), None),
            P(("frame", "tile"), None),
            P(("frame", "tile"), None),
            P(("frame", "tile"), None),
            P("frame", None),
            P("frame"),
        ),
        out_specs=(
            P(("frame", "tile"), None),
            P(("frame", "tile"), None),
            P(("frame", "tile"), None),
        ),
        check_vma=False,
    )
```

profile of v0, /device:TPU:1, one launch (start us, length us, event | category | flops | bytes accessed | tf_op | source)
XLA Modules:
  0.0 414.3 jit_solution(16001147600516263024)
XLA Ops:
  0.6 1.7 copy.37
  3.7 9.2 %all-to-all-start = ((bf16[128,32,128]{2,0,1:T(8,128)(2,1)}), bf16[128,32,128]{2,0,1:T(8,128)(2,1)S(1)}, u32[]{:S(2)}, u32[]{:S(2)}) async-start(bf16[128,32,128]{2,0,1:T(8,128)(2,1)} %copy.38), calls=%async_computation | async-start | bytes 2097152 | tf_op jit(solution)/shard_map/all_to_all | solution.py:50
  14.9 12.8 %all-to-all-done = bf16[128,32,128]{2,0,1:T(8,128)(2,1)S(1)} async-done(((bf16[128,32,128]{2,0,1:T(8,128)(2,1)}), bf16[128,32,128]{2,0,1:T(8,128)(2,1)S(1)}, u32[]{:S(2)}, u32[]{:S(2)}) %all-to-all-start) | async-done | bytes 1048608 | tf_op jit(solution)/shard_map/all_to_all | solution.py:50
  27.7 6.8 %all-to-all-start.2 = ((bf16[128,32,128]{2,0,1:T(8,128)(2,1)}), bf16[128,32,128]{2,0,1:T(8,128)(2,1)}, u32[]{:S(2)}, u32[]{:S(2)}) async-start(bf16[128,32,128]{2,0,1:T(8,128)(2,1)} %copy.46), calls=%async_computation.2 | async-start | bytes 2097152 | tf_op jit(solution)/shard_map/all_to_all | solution.py:51
  34.5 1.6 copy.41
  37.5 11.7 %all-to-all-done.2 = bf16[128,32,128]{2,0,1:T(8,128)(2,1)} async-done(((bf16[128,32,128]{2,0,1:T(8,128)(2,1)}), bf16[128,32,128]{2,0,1:T(8,128)(2,1)}, u32[]{:S(2)}, u32[]{:S(2)}) %all-to-all-start.2) | async-done | bytes 1048608 | tf_op jit(solution)/shard_map/all_to_all | solution.py:51
  49.2 6.9 %all-to-all-start.1 = ((bf16[128,32,128]{2,0,1:T(8,128)(2,1)}), bf16[128,32,128]{2,0,1:T(8,128)(2,1)}, u32[]{:S(2)}, u32[]{:S(2)}) async-start(bf16[128,32,128]{2,0,1:T(8,128)(2,1)} %copy.42), calls=%async_computation.1 | async-start | bytes 2097152 | tf_op jit(solution)/shard_map/all_to_all | solution.py:49
  56.1 3.1 collective-permute-start.1
  59.2 4.8 %collective-permute-start = (bf16[32,128,1,128]{3,1,0,2:T(8,128)(2,1)S(1)}, bf16[32,128,1,128]{3,1,0,2:T(8,128)(2,1)}, u32[]{:S(2)}, u32[]{:S(2)}) collective-permute-start(bf16[32,128,1,128]{3,1,0,2:T(8,128)(2,1)S(1)} %bitcast.150), channel_id=1, source_target_pairs={{0,32},{32,64},{64,96},{96,128},{128,160},{160,192},{192,224},{1,3... | collective-permute-start | bytes 3145736 | tf_op jit(solution)/shard_map/ppermute | solution.py:13
  64.0 1.9 collective-permute-start.3
  65.9 4.5 %collective-permute-start.2 = (bf16[32,128,1,128]{3,1,0,2:T(8,128)(2,1)}, bf16[32,128,1,128]{3,1,0,2:T(8,128)(2,1)}, u32[]{:S(2)}, u32[]{:S(2)}) collective-permute-start(bf16[32,128,1,128]{3,1,0,2:T(8,128)(2,1)} %bitcast.14), channel_id=1, source_target_pairs={{0,32},{32,64},{64,96},{96,128},{128,160},{160,192},{192,224},{1,3... | collective-permute-start | bytes 3145736 | tf_op jit(solution)/shard_map/ppermute | solution.py:13
  72.9 2.1 collective-permute-done.1
  75.0 4.0 collective-permute-done
  79.0 2.0 maximum_bitcast_fusion
  81.0 12.1 %all-to-all-done.1 = bf16[128,32,128]{2,0,1:T(8,128)(2,1)} async-done(((bf16[128,32,128]{2,0,1:T(8,128)(2,1)}), bf16[128,32,128]{2,0,1:T(8,128)(2,1)}, u32[]{:S(2)}, u32[]{:S(2)}) %all-to-all-start.1) | async-done | bytes 1048608 | tf_op jit(solution)/shard_map/all_to_all | solution.py:49
  93.2 22.4 %all-to-all-start.3 = ((bf16[128,32,128]{2,0,1:T(8,128)(2,1)}), bf16[128,32,128]{2,0,1:T(8,128)(2,1)}, u32[]{:S(2)}, u32[]{:S(2)}) async-start(bf16[128,32,128]{2,0,1:T(8,128)(2,1)} %copy.50), calls=%async_computation.3 | async-start | bytes 2097152 | tf_op jit(solution)/shard_map/all_to_all | solution.py:52
  115.6 3.3 maximum_bitcast_fusion.1
  118.9 8.1 %gather_fusion = bf16[192,128,128]{2,1,0:T(8,128)(2,1)} fusion(bf16[96,128,128]{2,1,0:T(8,128)(2,1)S(1)} %maximum_bitcast_fusion, s32[1024]{0:T(1024)S(1)} %pad_clamp_fusion), kind=kCustom, calls=%fused_computation.clone | custom fusion | bytes 12583680 | tf_op jit(solution)/shard_map/jit(_take)/gather | solution.py:17
  126.9 8.7 %copy.40 = bf16[32,6,128,1,128]{2,4,1,0,3:T(8,128)(2,1)} copy(bf16[32,6,128,1,128]{4,2,1,0,3:T(8,128)(2,1)} %bitcast.139) | data formatting | bytes 12582912 | tf_op jit(solution)/shard_map/jit(_take)/gather | solution.py:17
  135.7 8.1 %gather_fusion.1 = bf16[192,128,128]{2,1,0:T(8,128)(2,1)} fusion(bf16[96,128,128]{2,1,0:T(8,128)(2,1)S(1)} %copy-done.2, s32[1024]{0:T(1024)S(1)} %pad_clamp_fusion), kind=kCustom, calls=%fused_computation.1.clone | custom fusion | bytes 12583680 | tf_op jit(solution)/shard_map/jit(_take)/gather | solution.py:18
  143.7 8.7 %copy.48 = bf16[32,6,128,1,128]{2,4,1,0,3:T(8,128)(2,1)} copy(bf16[32,6,128,1,128]{4,2,1,0,3:T(8,128)(2,1)} %bitcast.138) | data formatting | bytes 12582912 | tf_op jit(solution)/shard_map/jit(_take)/gather | solution.py:18
  152.4 6.2 %bitcast_reduce_fusion = (f32[32,128]{1,0:T(8,128)S(1)}, f32[32,6,128,128]{3,2,1,0:T(8,128)S(1)}) fusion(pred[32,6]{1,0:T(8,128)(4,1)S(1)} %iota_compare_fusion, bf16[128,32,128]{2,0,1:T(8,128)(2,1)} %all-to-all-done.1, bf16[32,6,128,1,128]{2,4,1,0,3:T(8,128)(2,1)} %copy.40, pred[32,6]{1,0:T(8,128)(4,1)S(1)} %copy.36), kind=kOutput, calls=%fused_computation.5 | convolution fusion | flops 817885184 | bytes 19939712 | tf_op jit(solution)/shard_map/nahd,nsbhd->nhasb/dot_general | solution.py:21
  158.6 3.0 fusion.1
  161.6 1.5 copy-done
  163.2 9.6 %fusion.25 = f32[32,128]{1,0:T(8,128)S(1)} fusion(bf16[32,6,128,1,128]{2,4,1,0,3:T(8,128)(2,1)} %copy.48, pred[32,6]{1,0:T(8,128)(4,1)S(1)} %copy.36, bf16[128,32,128]{2,0,1:T(8,128)(2,1)} %all-to-all-done.3, f32[32,6,128,128]{3,2,1,0:T(8,128)} %copy-done, f32[32,128]{1,0:T(8,128)S(1)} %log_add_fusion, pred[32,6]{1,0:T(8,128)(4,1)S(1)} %iota_compare_fusion), kind=kOutput, calls=%fused_computation.39 | convolution fusion | flops 822603776 | bytes 19956096 | tf_op jit(solution)/shard_map/nhasb,nsbhd->nahd/dot_general | solution.py:30
  173.5 9.6 %fusion.4 = bf16[32,128,6,128]{1,3,2,0:T(8,128)(2,1)} fusion(f32[32,6,128,128]{3,2,1,0:T(8,128)S(1)} %copy-done.1, f32[32,128]{1,0:T(8,128)S(1)} %fusion.25, f32[32,128]{1,0:T(8,128)S(1)} %log_add_fusion, pred[32,6]{1,0:T(8,128)(4,1)S(1)} %iota_compare_fusion, bf16[32,6,128,1,128]{2,4,1,0,3:T(8,128)(2,1)} %copy.48, pred[32,6]{1,0:T(8,128)(4,1)S(1)} %copy.36, ...), kind=kOutput, calls=%fused_computation.12 | convolution fusion | flops 827326464 | bytes 26247552 | tf_op jit(solution)/shard_map/nahd,nsbhd->nhasb/dot_general | solution.py:32
  183.0 7.4 %fusion.31 = bf16[32,128,128]{1,2,0:T(8,128)(2,1)} fusion(bf16[32,128,6,128]{1,3,2,0:T(8,128)(2,1)} %fusion.4, bf16[32,6,128,1,128]{2,4,1,0,3:T(8,128)(2,1)} %copy.40, pred[32,6]{1,0:T(8,128)(4,1)S(1)} %copy.36), kind=kOutput, calls=%fused_computation.42 | convolution fusion | flops 809500672 | bytes 13631680 | tf_op jit(solution)/shard_map/nhasb,nsbhd->nahd/dot_general | solution.py:34
  190.5 14.1 %all-to-all-start.4 = ((bf16[32,128,128]{1,2,0:T(8,128)(2,1)}), bf16[32,128,128]{1,2,0:T(8,128)(2,1)S(1)}, u32[]{:S(2)}, u32[]{:S(2)}) async-start(bf16[32,128,128]{1,2,0:T(8,128)(2,1)} %fusion.31), calls=%async_computation.4 | async-start | bytes 2097152 | tf_op jit(solution)/shard_map/all_to_all | solution.py:86
  204.6 9.3 %fusion.39 = f32[32,6,128,128]{3,2,1,0:T(8,128)} fusion(bf16[32,128,6,128]{1,3,2,0:T(8,128)(2,1)} %fusion.4, bf16[128,32,128]{2,0,1:T(8,128)(2,1)} %all-to-all-done.1), kind=kOutput, calls=%fused_computation.52 | convolution fusion | flops 805306368 | bytes 19922944 | tf_op jit(solution)/shard_map/nhasb,nahd->nsbhd/dot_general | solution.py:35
  213.9 3.5 broadcast.72.clone
  217.4 39.6 %scatter_fusion = f32[96,128,128]{2,1,0:T(8,128)} fusion(f32[96,128,128]{2,1,0:T(8,128)} %broadcast.72.clone, s32[192]{0:T(256)S(1)} %reshape.217, f32[192,128,128]{2,1,0:T(8,128)} %bitcast.137), kind=kCustom, calls=%fused_computation.2 | custom fusion | flops 3145728 | bytes 37749504 | tf_op jit(solution)/shard_map/scatter-add | solution.py:41
  257.0 4.0 broadcast_multiply_fusion
  261.2 1.9 collective-permute-start.5
  263.1 2.5 collective-permute-start.4
  265.6 9.3 %collective-permute-done.5 = bf16[32,128,1,128]{3,1,0,2:T(8,128)(2,1)S(1)} collective-permute-done((bf16[32,128,1,128]{3,1,0,2:T(8,128)(2,1)S(1)}, bf16[32,128,1,128]{3,1,0,2:T(8,128)(2,1)S(1)}, u32[]{:S(2)}, u32[]{:S(2)}) %collective-permute-start.5) | collective-permute-done | bytes 1048608 | tf_op jit(solution)/shard_map/ppermute | solution.py:13
  274.9 18.3 %collective-permute-done.4 = bf16[32,128,1,128]{3,1,0,2:T(8,128)(2,1)S(1)} collective-permute-done((bf16[32,128,1,128]{3,1,0,2:T(8,128)(2,1)S(1)}, bf16[32,128,1,128]{3,1,0,2:T(8,128)(2,1)S(1)}, u32[]{:S(2)}, u32[]{:S(2)}) %collective-permute-start.4) | collective-permute-done | bytes 1048608 | tf_op jit(solution)/shard_map/ppermute | solution.py:13
  294.6 7.1 %all-to-all-start.5 = ((bf16[32,128,128]{2,1,0:T(8,128)(2,1)}), bf16[32,128,128]{2,1,0:T(8,128)(2,1)S(1)}, u32[]{:S(2)}, u32[]{:S(2)}) async-start(bf16[32,128,128]{2,1,0:T(8,128)(2,1)} %fusion.34), calls=%async_computation.5 | async-start | bytes 2097152 | tf_op jit(solution)/shard_map/all_to_all | solution.py:87
  301.7 11.4 %fusion.36 = f32[32,6,128,128]{3,2,1,0:T(8,128)} fusion(bf16[128,32,128]{2,0,1:T(8,128)(2,1)} %all-to-all-done.3, f32[32,6,128,128]{3,2,1,0:T(8,128)} %copy-done, f32[32,128]{1,0:T(8,128)S(1)} %log_add_fusion, pred[32,6]{1,0:T(8,128)(4,1)S(1)} %iota_compare_fusion), kind=kOutput, calls=%fused_computation.49 | convolution fusion | flops 817889280 | bytes 26230976 | tf_op jit(solution)/shard_map/nhasb,nahd->nsbhd/dot_general | solution.py:38
  313.1 3.5 broadcast.72.clone.1
  316.6 39.7 %scatter_fusion.1 = f32[96,128,128]{2,1,0:T(8,128)} fusion(f32[96,128,128]{2,1,0:T(8,128)} %broadcast.72.clone.1, s32[192]{0:T(256)S(1)} %reshape.217, f32[192,128,128]{2,1,0:T(8,128)} %bitcast.136), kind=kCustom, calls=%fused_computation.3 | custom fusion | flops 3145728 | bytes 37749504 | tf_op jit(solution)/shard_map/scatter-add | solution.py:42
  356.3 3.5 convert.12
  359.9 1.9 collective-permute-start.7
  361.8 2.5 collective-permute-start.6
  364.3 9.3 %collective-permute-done.7 = bf16[32,128,1,128]{3,1,0,2:T(8,128)(2,1)S(1)} collective-permute-done((bf16[32,128,1,128]{3,1,0,2:T(8,128)(2,1)S(1)}, bf16[32,128,1,128]{3,1,0,2:T(8,128)(2,1)S(1)}, u32[]{:S(2)}, u32[]{:S(2)}) %collective-permute-start.7) | collective-permute-done | bytes 1048608 | tf_op jit(solution)/shard_map/ppermute | solution.py:13
  373.6 17.4 %collective-permute-done.6 = bf16[32,128,1,128]{3,1,0,2:T(8,128)(2,1)S(1)} collective-permute-done((bf16[32,128,1,128]{3,1,0,2:T(8,128)(2,1)S(1)}, bf16[32,128,1,128]{3,1,0,2:T(8,128)(2,1)S(1)}, u32[]{:S(2)}, u32[]{:S(2)}) %collective-permute-start.6) | collective-permute-done | bytes 1048608 | tf_op jit(solution)/shard_map/ppermute | solution.py:13
  391.0 3.0 fusion.35
  394.0 6.8 %all-to-all-start.6 = ((bf16[32,128,128]{2,1,0:T(8,128)(2,1)}), bf16[32,128,128]{2,1,0:T(8,128)(2,1)S(1)}, u32[]{:S(2)}, u32[]{:S(2)}) async-start(bf16[32,128,128]{2,1,0:T(8,128)(2,1)} %fusion.35), calls=%async_computation.6 | async-start | bytes 2097152 | tf_op jit(solution)/shard_map/all_to_all | solution.py:88
  404.1 8.2 %all-to-all-done.6 = bf16[32,128,128]{2,1,0:T(8,128)(2,1)S(1)} async-done(((bf16[32,128,128]{2,1,0:T(8,128)(2,1)}), bf16[32,128,128]{2,1,0:T(8,128)(2,1)S(1)}, u32[]{:S(2)}, u32[]{:S(2)}) %all-to-all-start.6) | async-done | bytes 1048608 | tf_op jit(solution)/shard_map/all_to_all | solution.py:88
  (42 shorter events, 14.8 us)
Async XLA Ops:
  0.6 12.3 %copy-start.4 = (bf16[128,4096]{1,0:T(8,128)(2,1)S(1)}, bf16[128,4096]{1,0:T(8,128)(2,1)}, u32[]{:S(2)}) copy-start(bf16[128,4096]{1,0:T(8,128)(2,1)} %param.10) | copy-start | bytes 3145732
  3.7 24.1 %all-to-all-start = ((bf16[128,32,128]{2,0,1:T(8,128)(2,1)}), bf16[128,32,128]{2,0,1:T(8,128)(2,1)S(1)}, u32[]{:S(2)}, u32[]{:S(2)}) async-start(bf16[128,32,128]{2,0,1:T(8,128)(2,1)} %copy.38), calls=%async_computation | async-start | bytes 2097152 | tf_op jit(solution)/shard_map/all_to_all | solution.py:50
  12.9 57.6 %copy-start.6 = (s32[32,6]{0,1:T(8,128)S(1)}, s32[32,6]{0,1:T(8,128)}, u32[]{:S(2)}) copy-start(s32[32,6]{0,1:T(8,128)} %param.12) | copy-start | bytes 2308
  13.6 57.2 %copy-start.5 = (bf16[128,4096]{1,0:T(8,128)(2,1)S(1)}, bf16[128,4096]{1,0:T(8,128)(2,1)}, u32[]{:S(2)}) copy-start(bf16[128,4096]{1,0:T(8,128)(2,1)} %param.11) | copy-start | bytes 3145732
  14.9 57.9 %copy-start.7 = (s32[32]{0:T(128)S(1)}, s32[32]{0:T(128)}, u32[]{:S(2)}) copy-start(s32[32]{0:T(128)} %param.13) | copy-start | bytes 388
  27.7 45.1 %copy-start.3 = (bf16[128,32,128]{2,0,1:T(8,128)(2,1)}, bf16[128,32,128]{2,0,1:T(8,128)(2,1)S(1)}, u32[]{:S(2)}) copy-start(bf16[128,32,128]{2,0,1:T(8,128)(2,1)S(1)} %all-to-all-done) | copy-start | bytes 3145732
  27.7 21.4 %all-to-all-start.2 = ((bf16[128,32,128]{2,0,1:T(8,128)(2,1)}), bf16[128,32,128]{2,0,1:T(8,128)(2,1)}, u32[]{:S(2)}, u32[]{:S(2)}) async-start(bf16[128,32,128]{2,0,1:T(8,128)(2,1)} %copy.46), calls=%async_computation.2 | async-start | bytes 2097152 | tf_op jit(solution)/shard_map/all_to_all | solution.py:51
  49.2 44.0 %all-to-all-start.1 = ((bf16[128,32,128]{2,0,1:T(8,128)(2,1)}), bf16[128,32,128]{2,0,1:T(8,128)(2,1)}, u32[]{:S(2)}, u32[]{:S(2)}) async-start(bf16[128,32,128]{2,0,1:T(8,128)(2,1)} %copy.42), calls=%async_computation.1 | async-start | bytes 2097152 | tf_op jit(solution)/shard_map/all_to_all | solution.py:49
  56.1 18.9 %collective-permute-start.1 = (bf16[32,128,1,128]{3,1,0,2:T(8,128)(2,1)S(1)}, bf16[32,128,1,128]{3,1,0,2:T(8,128)(2,1)}, u32[]{:S(2)}, u32[]{:S(2)}) collective-permute-start(bf16[32,128,1,128]{3,1,0,2:T(8,128)(2,1)S(1)} %bitcast.149), channel_id=1, source_target_pairs={{32,0},{64,32},{96,64},{128,96},{160,128},{192,160},{224,192},{33,... | collective-permute-start | bytes 3145736 | tf_op jit(solution)/shard_map/ppermute | solution.py:13
  59.2 19.8 %collective-permute-start = (bf16[32,128,1,128]{3,1,0,2:T(8,128)(2,1)S(1)}, bf16[32,128,1,128]{3,1,0,2:T(8,128)(2,1)}, u32[]{:S(2)}, u32[]{:S(2)}) collective-permute-start(bf16[32,128,1,128]{3,1,0,2:T(8,128)(2,1)S(1)} %bitcast.150), channel_id=1, source_target_pairs={{0,32},{32,64},{64,96},{96,128},{128,160},{160,192},{192,224},{1,3... | collective-permute-start | bytes 3145736 | tf_op jit(solution)/shard_map/ppermute | solution.py:13
  64.0 51.5 %collective-permute-start.3 = (bf16[32,128,1,128]{3,1,0,2:T(8,128)(2,1)}, bf16[32,128,1,128]{3,1,0,2:T(8,128)(2,1)}, u32[]{:S(2)}, u32[]{:S(2)}) collective-permute-start(bf16[32,128,1,128]{3,1,0,2:T(8,128)(2,1)} %bitcast.14), channel_id=1, source_target_pairs={{32,0},{64,32},{96,64},{128,96},{160,128},{192,160},{224,192},{33,... | collective-permute-start | bytes 3145736 | tf_op jit(solution)/shard_map/ppermute | solution.py:13
  65.9 49.6 %collective-permute-start.2 = (bf16[32,128,1,128]{3,1,0,2:T(8,128)(2,1)}, bf16[32,128,1,128]{3,1,0,2:T(8,128)(2,1)}, u32[]{:S(2)}, u32[]{:S(2)}) collective-permute-start(bf16[32,128,1,128]{3,1,0,2:T(8,128)(2,1)} %bitcast.14), channel_id=1, source_target_pairs={{0,32},{32,64},{64,96},{96,128},{128,160},{160,192},{192,224},{1,3... | collective-permute-start | bytes 3145736 | tf_op jit(solution)/shard_map/ppermute | solution.py:13
  93.2 70.0 %all-to-all-start.3 = ((bf16[128,32,128]{2,0,1:T(8,128)(2,1)}), bf16[128,32,128]{2,0,1:T(8,128)(2,1)}, u32[]{:S(2)}, u32[]{:S(2)}) async-start(bf16[128,32,128]{2,0,1:T(8,128)(2,1)} %copy.50), calls=%async_computation.3 | async-start | bytes 2097152 | tf_op jit(solution)/shard_map/all_to_all | solution.py:52
  126.9 8.7 %copy-start.2 = (bf16[96,128,128]{2,1,0:T(8,128)(2,1)S(1)}, bf16[96,128,128]{2,1,0:T(8,128)(2,1)}, u32[]{:S(2)}) copy-start(bf16[96,128,128]{2,1,0:T(8,128)(2,1)} %maximum_bitcast_fusion.1) | copy-start | bytes 9437188
  158.6 4.5 %copy-start = (f32[32,6,128,128]{3,2,1,0:T(8,128)}, f32[32,6,128,128]{3,2,1,0:T(8,128)S(1)}, u32[]{:S(2)}) copy-start(f32[32,6,128,128]{3,2,1,0:T(8,128)S(1)} %get-tuple-element.20) | copy-start | bytes 37748740
  163.2 10.3 %copy-start.1 = (f32[32,6,128,128]{3,2,1,0:T(8,128)S(1)}, f32[32,6,128,128]{3,2,1,0:T(8,128)}, u32[]{:S(2)}) copy-start(f32[32,6,128,128]{3,2,1,0:T(8,128)} %copy-done) | copy-start | bytes 37748740
  190.5 104.2 %all-to-all-start.4 = ((bf16[32,128,128]{1,2,0:T(8,128)(2,1)}), bf16[32,128,128]{1,2,0:T(8,128)(2,1)S(1)}, u32[]{:S(2)}, u32[]{:S(2)}) async-start(bf16[32,128,128]{1,2,0:T(8,128)(2,1)} %fusion.31), calls=%async_computation.4 | async-start | bytes 2097152 | tf_op jit(solution)/shard_map/all_to_all | solution.py:86
  261.2 13.7 %collective-permute-start.5 = (bf16[32,128,1,128]{3,1,0,2:T(8,128)(2,1)S(1)}, bf16[32,128,1,128]{3,1,0,2:T(8,128)(2,1)S(1)}, u32[]{:S(2)}, u32[]{:S(2)}) collective-permute-start(bf16[32,128,1,128]{3,1,0,2:T(8,128)(2,1)S(1)} %get-tuple-element.18), channel_id=1, source_target_pairs={{0,32},{32,64},{64,96},{96,128},{128,160},{160,192},{192,224},{1,3... | collective-permute-start | bytes 3145736 | tf_op jit(solution)/shard_map/ppermute | solution.py:13
  263.1 30.1 %collective-permute-start.4 = (bf16[32,128,1,128]{3,1,0,2:T(8,128)(2,1)S(1)}, bf16[32,128,1,128]{3,1,0,2:T(8,128)(2,1)S(1)}, u32[]{:S(2)}, u32[]{:S(2)}) collective-permute-start(bf16[32,128,1,128]{3,1,0,2:T(8,128)(2,1)S(1)} %get-tuple-element.17), channel_id=1, source_target_pairs={{32,0},{64,32},{96,64},{128,96},{160,128},{192,160},{224,192},{33,... | collective-permute-start | bytes 3145736 | tf_op jit(solution)/shard_map/ppermute | solution.py:13
  294.6 99.4 %all-to-all-start.5 = ((bf16[32,128,128]{2,1,0:T(8,128)(2,1)}), bf16[32,128,128]{2,1,0:T(8,128)(2,1)S(1)}, u32[]{:S(2)}, u32[]{:S(2)}) async-start(bf16[32,128,128]{2,1,0:T(8,128)(2,1)} %fusion.34), calls=%async_computation.5 | async-start | bytes 2097152 | tf_op jit(solution)/shard_map/all_to_all | solution.py:87
  359.9 13.7 %collective-permute-start.7 = (bf16[32,128,1,128]{3,1,0,2:T(8,128)(2,1)S(1)}, bf16[32,128,1,128]{3,1,0,2:T(8,128)(2,1)S(1)}, u32[]{:S(2)}, u32[]{:S(2)}) collective-permute-start(bf16[32,128,1,128]{3,1,0,2:T(8,128)(2,1)S(1)} %get-tuple-element.16), channel_id=1, source_target_pairs={{0,32},{32,64},{64,96},{96,128},{128,160},{160,192},{192,224},{1,3... | collective-permute-start | bytes 3145736 | tf_op jit(solution)/shard_map/ppermute | solution.py:13
  361.8 29.1 %collective-permute-start.6 = (bf16[32,128,1,128]{3,1,0,2:T(8,128)(2,1)S(1)}, bf16[32,128,1,128]{3,1,0,2:T(8,128)(2,1)S(1)}, u32[]{:S(2)}, u32[]{:S(2)}) collective-permute-start(bf16[32,128,1,128]{3,1,0,2:T(8,128)(2,1)S(1)} %get-tuple-element.15), channel_id=1, source_target_pairs={{32,0},{64,32},{96,64},{128,96},{160,128},{192,160},{224,192},{33,... | collective-permute-start | bytes 3145736 | tf_op jit(solution)/shard_map/ppermute | solution.py:13
  394.0 18.3 %all-to-all-start.6 = ((bf16[32,128,128]{2,1,0:T(8,128)(2,1)}), bf16[32,128,128]{2,1,0:T(8,128)(2,1)S(1)}, u32[]{:S(2)}, u32[]{:S(2)}) async-start(bf16[32,128,128]{2,1,0:T(8,128)(2,1)} %fusion.35), calls=%async_computation.6 | async-start | bytes 2097152 | tf_op jit(solution)/shard_map/all_to_all | solution.py:88
where the time goes:
time: 419 us; the launch traced here: 414 us
  waiting for transfers between devices  105 us (25%)
  other arithmetic  99.6 us (24%)
  starting transfers between devices  96.4 us (23%)
  local copies, waits for them, and re-layouts  58.6 us (14%)
  matrix products  53.5 us (13%)
    ppermute x8, waiting for transfers between devices, shifted(): return lax.ppermute(array, axis, pairs)  60.3 us
    scatter-add x1, other arithmetic, attend_back(): dv = jnp.zeros(k_all.shape, jnp.float32).at[lists].add(value_terms)  39.7 us
    scatter-add x1, other arithmetic, attend_back(): dk = jnp.zeros(k_all.shape, jnp.float32).at[lists].add(key_terms)  39.6 us
    ppermute x8, starting transfers between devices, shifted(): return lax.ppermute(array, axis, pairs)  23.1 us
    all_to_all x1, starting transfers between devices, local(): lax.all_to_all(out_grad, 'tile', split_axis=1, concat_axis=0, tiled=True)  22.4 us
    gather x2, local copies, waits for them, and re-layouts, attend_back(): k_listed = jnp.take(k_all, lists, axis=0)  16.8 us
    gather x2, local copies, waits for them, and re-layouts, attend_back(): v_listed = jnp.take(v_all, lists, axis=0)  16.8 us
    all_to_all x1, starting transfers between devices, local(): lax.all_to_all(flat(dq), 'tile', split_axis=0, concat_axis=1, tiled=True)  14.1 us
  transfers between devices with their start and end apart: 15, of which 10 were waited for; matrix products, arithmetic and copies ran while one was open for 43% of the time, Pallas kernels for 0%

commit v1 on v0

v1 whole, which is shorter than its diff:
```python
import functools

import jax
import jax.numpy as jnp
from jax import lax
from jax.experimental import pallas as pl
from jax.experimental.pallas import tpu as pltpu
from jax.sharding import PartitionSpec as P

D = 128
NEAR = 16
MESH = pl.DeviceIdType.MESH
ANY = pl.BlockSpec(memory_space=pl.ANY)
SMEM = pl.BlockSpec(memory_space=pltpu.SMEM)
VMEM = pl.BlockSpec(memory_space=pltpu.VMEM)
LOG2E = 1.4426950408889634


def peer_of(i, me, tiles):
    half = tiles // 2
    z, y, x = me // half, (me % half) // 4, me % 4
    z = (z + i) % 2
    x = (x + i // 2) % 4
    y = (y + i // 8) % (half // 4)
    return z * half + y * 4 + x


def greet(tiles, me, before, after):
    barrier = pltpu.get_barrier_semaphore()

    def hello(i, carry):
        pl.semaphore_signal(barrier, inc=1, device_id={"tile": peer_of(i, me, tiles)}, device_id_type=MESH)
        return carry

    lax.fori_loop(1, tiles, hello, 0)
    for frame in (before, after):
        pl.semaphore_signal(barrier, inc=1, device_id={"frame": frame}, device_id_type=MESH)
    pl.semaphore_wait(barrier, tiles + 1)


def wait_bytes(ref, sem):
    pltpu.make_async_copy(ref, ref, sem).wait()


def gather_kernel(tiles, frames, pick_ref, q_ref, k_ref, v_ref, g_ref, q_out, g_out, kv_out,
                  own, packed, send_sem, recv_sem, local_sem, near_send, near_recv):
    me, frame = lax.axis_index("tile"), lax.axis_index("frame")
    before, after = (frame + frames - 1) % frames, (frame + 1) % frames
    greet(tiles, me, before, after)

    places = (
        (k_ref, lambda t: own.at[t, :, pl.ds(0, D)]),
        (v_ref, lambda t: own.at[t, :, pl.ds(D, D)]),
        (q_ref, lambda t: q_out.at[t]),
        (g_ref, lambda t: g_out.at[t]),
    )
    for a, (src, place) in enumerate(places):
        def send(i, carry, a=a, src=src, place=place):
            to = peer_of(i, me, tiles)
            pltpu.make_async_remote_copy(
                src_ref=src.at[:, pl.ds(pl.multiple_of(to * D, D), D)], dst_ref=place(me),
                send_sem=send_sem.at[a], recv_sem=recv_sem.at[a],
                device_id={"tile": to}, device_id_type=MESH,
            ).start()
            return carry

        lax.fori_loop(1, tiles, send, 0)
        pltpu.make_async_copy(
            src.at[:, pl.ds(pl.multiple_of(me * D, D), D)], place(me), local_sem.at[a]
        ).start()

    for a in range(2):
        wait_bytes(own.at[pl.ds(0, tiles - 1), :, pl.ds(0, D)], recv_sem.at[a])
        pltpu.make_async_copy(
            places[a][0].at[:, pl.ds(pl.multiple_of(me * D, D), D)], places[a][1](me), local_sem.at[a]
        ).wait()

    keep = pltpu.make_async_copy(own, kv_out.at[pl.ds(0, tiles)], local_sem.at[4])
    keep.start()
    near = []
    for side, frame_to in ((0, before), (1, after)):
        def pack(n, carry, side=side):
            packed[side, n] = own[pick_ref[side * NEAR + n]]
            return carry

        lax.fori_loop(0, NEAR, pack, 0)
        copy = pltpu.make_async_remote_copy(
            src_ref=packed.at[side], dst_ref=kv_out.at[pl.ds(tiles + (1 - side) * NEAR, NEAR)],
            send_sem=near_send.at[side], recv_sem=near_recv.at[side],
            device_id={"frame": frame_to}, device_id_type=MESH,
        )
        copy.start()
        near.append(copy)

    for a in range(2, 4):
        wait_bytes(q_out.at[pl.ds(0, tiles - 1)], recv_sem.at[a])
        pltpu.make_async_copy(
            places[a][0].at[:, pl.ds(pl.multiple_of(me * D, D), D)], places[a][1](me), local_sem.at[a]
        ).wait()
    for a in range(4):
        wait_bytes(q_out.at[pl.ds(0, tiles - 1)], send_sem.at[a])
    keep.wait()
    for copy in near:
        copy.wait()


def gather(tiles, frames, pick, q, k, v, g):
    bf16 = jnp.bfloat16
    return pl.pallas_call(
        functools.partial(gather_kernel, tiles, frames),
        out_shape=(
            jax.ShapeDtypeStruct((tiles, D, D), bf16),
            jax.ShapeDtypeStruct((tiles, D, D), bf16),
            jax.ShapeDtypeStruct((tiles + 2 * NEAR, D, 2 * D), bf16),
        ),
        in_specs=[SMEM, ANY, ANY, ANY, ANY],
        out_specs=(ANY, ANY, ANY),
        scratch_shapes=[
            pltpu.VMEM((tiles, D, 2 * D), bf16),
            pltpu.VMEM((2, NEAR, D, 2 * D), bf16),
            pltpu.SemaphoreType.DMA((4,)),
            pltpu.SemaphoreType.DMA((4,)),
            pltpu.SemaphoreType.DMA((5,)),
            pltpu.SemaphoreType.DMA((2,)),
            pltpu.SemaphoreType.DMA((2,)),
        ],
        compiler_params=pltpu.CompilerParams(
            collective_id=0, has_side_effects=True, vmem_limit_bytes=32 * 2**20
        ),
        name="gather",
    )(pick, q, k, v, g)


def attend_kernel(lists_ref, counts_ref, q_ref, g_ref, kv_ref, dq_ref, own_ref, near_ref, kt, acc):
    nblk = q_ref.shape[0]
    slots = lists_ref.shape[1]
    nkey = kv_ref.shape[0]
    scale = D ** (-0.5)

    def prepare(j, carry):
        kt[j] = kv_ref[j, :, 0:D].T
        acc[j] = jnp.zeros_like(acc[j])
        return carry

    lax.fori_loop(0, nkey, prepare, 0)

    def block(r, carry):
        q, g = q_ref[r], g_ref[r]
        zero = jnp.zeros_like(q)
        both = jnp.concatenate([jnp.concatenate([q, zero], 1), jnp.concatenate([zero, g], 1)], 0)
        count = counts_ref[r]
        idx = [lists_ref[r, s] for s in range(slots)]
        score, dprob, top = [], [], None
        for s in range(slots):
            out = lax.dot_general(
                kv_ref[idx[s]], both, (((1,), (1,)), ((), ())), preferred_element_type=jnp.float32
            )
            sc = out[:, :D] * (scale * LOG2E)
            if s >= 2:
                sc = jnp.where(s < count, sc, -1e30)
            score.append(sc)
            dprob.append(out[:, D:])
            high = jnp.max(sc, axis=0, keepdims=True)
            top = high if top is None else jnp.maximum(top, high)
        total = 0.0
        for s in range(slots):
            score[s] = jnp.exp2(score[s] - top)
            total = total + jnp.sum(score[s], axis=0, keepdims=True)
        inverse = 1.0 / total
        delta = 0.0
        low = []
        for s in range(slots):
            score[s] = score[s] * inverse
            low.append(score[s].astype(jnp.bfloat16))
            delta = delta + jnp.sum(low[s].astype(jnp.float32) * dprob[s], axis=0, keepdims=True)
        dlow = []
        for s in range(slots):
            dlow.append((score[s] * (dprob[s] - delta)).astype(jnp.bfloat16))
            terms = jnp.dot(
                jnp.concatenate([dlow[s], low[s]], 1), both, preferred_element_type=jnp.float32
            )
            acc[idx[s]] += terms
        dq = jnp.dot(
            jnp.concatenate([kt[idx[s]] for s in range(slots)], 1), jnp.concatenate(dlow, 0),
            preferred_element_type=jnp.float32,
        )
        dq_ref[r] = (dq * scale).T.astype(jnp.bfloat16)
        return carry

    lax.fori_loop(0, nblk, block, 0)

    def finish(j, carry):
        own_ref[j, :, 0:D] = acc[j, :, 0:D] * scale
        own_ref[j, :, D : 2 * D] = acc[j, :, D : 2 * D]
        near_ref[j, :, 0:D] = (acc[nblk + j, :, 0:D] * scale).astype(jnp.bfloat16)
        near_ref[j, :, D : 2 * D] = acc[nblk + j, :, D : 2 * D].astype(jnp.bfloat16)
        return carry

    lax.fori_loop(0, nblk, finish, 0)


def attend(lists, counts, q, g, kv):
    nblk, nkey = q.shape[0], kv.shape[0]
    bf16, f32 = jnp.bfloat16, jnp.float32
    return pl.pallas_call(
        attend_kernel,
        out_shape=(
            jax.ShapeDtypeStruct((nblk, D, D), bf16),
            jax.ShapeDtypeStruct((nblk, D, 2 * D), f32),
            jax.ShapeDtypeStruct((2 * NEAR, D, 2 * D), bf16),
        ),
        in_specs=[SMEM, SMEM, VMEM, VMEM, VMEM],
        out_specs=(VMEM, VMEM, VMEM),
        scratch_shapes=[pltpu.VMEM((nkey, D, D), bf16), pltpu.VMEM((nkey, D, 2 * D), f32)],
        compiler_params=pltpu.CompilerParams(vmem_limit_bytes=56 * 2**20),
        name="attend",
    )(lists, counts, q, g, kv)


def scatter_kernel(tiles, frames, named_ref, rank_ref, dq_ref, own_ref, part_ref, dq_out, dk_out, dv_out,
                   own, parts, total, send_sem, recv_sem, local_sem, near_send, near_recv):
    me, frame = lax.axis_index("tile"), lax.axis_index("frame")
    before, after = (frame + frames - 1) % frames, (frame + 1) % frames
    greet(tiles, me, before, after)
    mine = pl.ds(pl.multiple_of(me * D, D), D)

    load = pltpu.make_async_copy(own_ref, own, local_sem.at[3])
    load.start()
    near = []
    for side, frame_to in ((0, before), (1, after)):
        copy = pltpu.make_async_remote_copy(
            src_ref=part_ref.at[pl.ds(side * NEAR, NEAR)], dst_ref=parts.at[1 - side],
            send_sem=near_send.at[side], recv_sem=near_recv.at[side],
            device_id={"frame": frame_to}, device_id_type=MESH,
        )
        copy.start()
        near.append(copy)

    def send_dq(i, carry):
        to = peer_of(i, me, tiles)
        pltpu.make_async_remote_copy(
            src_ref=dq_ref.at[to], dst_ref=dq_out.at[:, mine],
            send_sem=send_sem.at[0], recv_sem=recv_sem.at[0],
            device_id={"tile": to}, device_id_type=MESH,
        ).start()
        return carry

    lax.fori_loop(1, tiles, send_dq, 0)
    local = [pltpu.make_async_copy(dq_ref.at[me], dq_out.at[:, mine], local_sem.at[0])]
    local[0].start()
    load.wait()
    for copy in near:
        copy.wait()

    def add(to):
        value = own[to]
        for side in range(2):
            at = side * tiles + to
            part = parts[side, rank_ref[at]].astype(jnp.float32)
            value = value + jnp.where(named_ref[at] > 0, part, 0.0)
        total[to] = value.astype(jnp.bfloat16)

    def send(i, carry):
        to = peer_of(i, me, tiles)
        add(to)
        for a, out in ((1, dk_out), (2, dv_out)):
            pltpu.make_async_remote_copy(
                src_ref=total.at[to, :, pl.ds((a - 1) * D, D)], dst_ref=out.at[:, mine],
                send_sem=send_sem.at[a], recv_sem=recv_sem.at[a],
                device_id={"tile": to}, device_id_type=MESH,
            ).start()
        return carry

    lax.fori_loop(1, tiles, send, 0)
    add(me)
    for a, out in ((1, dk_out), (2, dv_out)):
        copy = pltpu.make_async_copy(total.at[me, :, pl.ds((a - 1) * D, D)], out.at[:, mine], local_sem.at[a])
        copy.start()
        local.append(copy)
    for copy in local:
        copy.wait()
    for a in range(3):
        wait_bytes(dq_out.at[:, pl.ds(0, (tiles - 1) * D)], recv_sem.at[a])
        wait_bytes(dq_out.at[:, pl.ds(0, (tiles - 1) * D)], send_sem.at[a])


def scatter(tiles, frames, named, rank, dq, own, part):
    bf16 = jnp.bfloat16
    out = jax.ShapeDtypeStruct((D, tiles * D), bf16)
    return pl.pallas_call(
        functools.partial(scatter_kernel, tiles, frames),
        out_shape=(out, out, out),
        in_specs=[SMEM, SMEM, ANY, ANY, ANY],
        out_specs=(ANY, ANY, ANY),
        scratch_shapes=[
            pltpu.VMEM((tiles, D, 2 * D), jnp.float32),
            pltpu.VMEM((2, NEAR, D, 2 * D), bf16),
            pltpu.VMEM((tiles, D, 2 * D), bf16),
            pltpu.SemaphoreType.DMA((3,)),
            pltpu.SemaphoreType.DMA((3,)),
            pltpu.SemaphoreType.DMA((4,)),
            pltpu.SemaphoreType.DMA((2,)),
            pltpu.SemaphoreType.DMA((2,)),
        ],
        compiler_params=pltpu.CompilerParams(
            collective_id=1, has_side_effects=True, vmem_limit_bytes=32 * 2**20
        ),
        name="scatter",
    )(named, rank, dq, own, part)


def naming(lists, start, nblk):
    ids = jnp.arange(nblk, dtype=jnp.int32)
    named = jnp.any(lists.reshape(-1)[:, None] == ids[None, :] + start, axis=0)
    rank = jnp.sum(jnp.where((ids[:, None] < ids[None, :]) & named[:, None], 1, 0), axis=0).astype(jnp.int32)
    return named.astype(jnp.int32), jnp.minimum(rank, NEAR - 1)


def picks(named, rank):
    ids = jnp.arange(named.shape[0], dtype=jnp.int32)
    slot = jnp.arange(NEAR, dtype=jnp.int32)
    hit = (named[None, :] > 0) & (rank[None, :] == slot[:, None])
    return jnp.sum(jnp.where(hit, ids[None, :], 0), axis=1).astype(jnp.int32)


def compact(lists, nblk):
    (_, before), (_, after) = naming(lists, 0, nblk), naming(lists, 2 * nblk, nblk)
    place = jnp.concatenate([nblk + before, jnp.arange(nblk, dtype=jnp.int32), nblk + NEAR + after])
    hit = lists[:, :, None] == jnp.arange(3 * nblk, dtype=jnp.int32)
    return jnp.sum(jnp.where(hit, place, 0), axis=2).astype(jnp.int32)


def local(tiles, frames, queries, keys, values, out_grad, key_lists, key_counts):
    nblk = key_lists.shape[0]
    of_before = lax.ppermute(key_lists, "frame", [(i, (i + 1) % frames) for i in range(frames)])
    of_after = lax.ppermute(key_lists, "frame", [(i, (i - 1) % frames) for i in range(frames)])
    named_before, rank_before = naming(of_before, 2 * nblk, nblk)
    named_after, rank_after = naming(of_after, 0, nblk)
    pick = jnp.concatenate([picks(named_before, rank_before), picks(named_after, rank_after)])
    named = jnp.concatenate([named_before, named_after])
    rank = jnp.concatenate([rank_before, rank_after])

    q, g, kv = gather(tiles, frames, pick, queries, keys, values, out_grad)
    dq, own, part = attend(compact(key_lists, nblk), key_counts, q, g, kv)
    return scatter(tiles, frames, named, rank, dq, own, part)


def solution(mesh):
    both = P(("frame", "tile"), None)
    return jax.shard_map(
        functools.partial(local, mesh.shape["tile"], mesh.shape["frame"]),
        mesh=mesh,
        in_specs=(both, both, both, both, P("frame", None), P("frame")),
        out_specs=(both, both, both),
        check_vma=False,
    )
```

time: 419 us -> 216 us (0.52)
  Pallas kernels: 0 us -> 185 us
  waiting for transfers between devices: 105 us -> 2.33 us
  other arithmetic: 99.6 us -> 2.08 us
  starting transfers between devices: 96.4 us -> 4.55 us
  matrix products: 53.5 us -> 0 us
  local copies, waits for them, and re-layouts: 58.6 us -> 18.6 us
    pallas_call x0 -> x3, Pallas kernels: none -> 185 us  [the longest x1 75.3 us: gather(): pl.pallas_call(functools.partial(gather_kernel, tiles, frames), out_shape...]
    scatter-add x2 -> x0, other arithmetic: 79.3 us -> none  [the longest x1 39.7 us: attend_back(): dv = jnp.zeros(k_all.shape, jnp.float32).at[lists].add(value_terms)]
    all_to_all x7 -> x0, starting transfers between devices: 73.3 us -> none  [the longest x1 22.4 us: local(): lax.all_to_all(out_grad, 'tile', split_axis=1, concat_axis=0, tiled=True)]
    ppermute x8 -> x2, waiting for transfers between devices: 60.3 us -> 2.33 us  [the longest x1 1.82 us: local(): lax.ppermute(key_lists, 'frame', [(i, (i + 1) % frames) for i in range(fr...]
    dot_general x6 -> x0, matrix products: 53.5 us -> none  [the longest x1 11.4 us: attend_back(): jnp.einsum('nhasb,nahd->nsbhd', plow, g_blocks, preferred_element_type=jn...]
    all_to_all x7 -> x0, waiting for transfers between devices: 44.9 us -> none  [the longest x1 12.8 us: local(): lax.all_to_all(keys, 'tile', split_axis=1, concat_axis=0, tiled=True)]
    gather x4 -> x0, local copies, waits for them, and re-layouts: 33.5 us -> none  [the longest x2 16.8 us: attend_back(): k_listed = jnp.take(k_all, lists, axis=0)]
    ppermute x8 -> x2, starting transfers between devices: 23.1 us -> 4.55 us  [the longest x1 3.32 us: local(): lax.ppermute(key_lists, 'frame', [(i, (i - 1) % frames) for i in range(fr...]
  transfers between devices with their start and end apart: 15 -> 2, of which waited for: 10 -> 2; matrix products, arithmetic and copies ran while one was open for 43% -> 1% of each run, Pallas kernels for 0% -> 0%
where the time goes in v1:
time: 216 us; the launch traced here: 213 us
  Pallas kernels  185 us (86%)
  local copies, waits for them, and re-layouts  18.6 us (9%)
  starting transfers between devices  4.55 us (2%)
  waiting for transfers between devices  2.33 us (1%)
    pallas_call x1, Pallas kernels, gather(): pl.pallas_call(functools.partial(gather_kernel, tiles, frames), out_shape...  75.3 us
    pallas_call x1, Pallas kernels, scatter(): pl.pallas_call(functools.partial(scatter_kernel, tiles, frames), out_shap...  67.5 us
    pallas_call x1, Pallas kernels, attend(): pl.pallas_call(attend_kernel, out_shape=(jax.ShapeDtypeStruct((nblk, D, D...  42.3 us
    unnamed x24, local copies, waits for them, and re-layouts  17.5 us
  transfers between devices with their start and end apart: 2, of which 2 were waited for; matrix products, arithmetic and copies ran while one was open for 1% of the time, Pallas kernels for 0%

profile of v1, /device:TPU:1, one launch (start us, length us, event | category | flops | bytes accessed | tf_op | source)
XLA Modules:
  0.0 213.4 jit_solution(6024253085351076978)
XLA Ops:
  0.6 3.3 %collective-permute-start.1 = (s32[32,6]{0,1:T(8,128)}, s32[32,6]{0,1:T(8,128)S(1)}, u32[]{:S(2)}, u32[]{:S(2)}) collective-permute-start(s32[32,6]{0,1:T(8,128)} %param.10), channel_id=1, source_target_pairs={{0,224},{32,0},{64,32},{96,64},{128,96},{160,128},{192,160},{224,1... | collective-permute-start | bytes 2312 | tf_op jit(solution)/shard_map/ppermute | solution.py:336
  3.9 1.2 collective-permute-start
  5.2 0.8 copy.16
  6.0 0.1 eq.106
  6.1 0.5 collective-permute-done.1
  6.6 0.1 copy.15
  6.7 0.1 eq.99
  6.8 0.1 fusion
  6.9 0.1 select_reduce_fusion.3
  7.0 1.8 collective-permute-done
  8.8 0.1 copy.14
  8.9 0.1 eq.46
  9.0 0.2 fusion.1
  9.2 0.1 select_reduce_fusion.4
  9.3 0.1 select_reduce_fusion.1
  9.4 0.1 pad_add_fusion.1.rank_ref
  9.5 0.1 select_reduce_fusion.6
  9.6 0.1 select_reduce_fusion.5
  9.8 0.1 pad_add_fusion.2
  9.8 0.9 select_reduce_fusion
  10.8 0.7 copy.17.lists_ref
  11.5 0.1 pad_add_fusion.3.pick_ref
  11.5 0.1 pad_add_fusion.named_ref
  11.6 0.0 copy-start.3
  11.6 1.2 copy-done.3
  12.8 0.0 copy-start.4
  12.8 1.2 copy-done.4
  14.1 0.0 copy-start.5
  14.1 1.2 copy-done.5
  15.3 0.0 copy-start.6
  15.3 1.2 copy-done.6
  16.5 75.3 %gather.1 = (bf16[32,128,128]{2,1,0:T(8,128)(2,1)S(1)}, bf16[32,128,128]{2,1,0:T(8,128)(2,1)S(1)}, bf16[64,128,256]{2,1,0:T(8,128)(2,1)S(1)}) custom-call(s32[32]{0:T(128)S(1)} %pad_add_fusion.3.pick_ref, bf16[128,4096]{1,0:T(8,128)(2,1)S(1)} %copy-done.3, bf16[128,4096]{1,0:T(8,128)(2,1)S(1)} %copy-done.4, bf16[128,4096]{1,0:T(8,128)(2,1)S(1)} %copy-done.5, ...), custom_call_target="tpu_custom_call" | custom-call | tf_op jit(solution)/shard_map/gather/pallas_call | solution.py:109
  91.8 0.0 copy-start
  91.9 1.9 copy-done
  93.8 0.0 copy-start.7
  93.8 1.0 copy-done.7
  94.7 0.0 copy-start.8
  94.7 1.0 copy-done.8
  95.7 42.3 %attend.1 = (bf16[32,128,128]{2,1,0:T(8,128)(2,1)}, f32[32,128,256]{2,1,0:T(8,128)}, bf16[32,128,256]{2,1,0:T(8,128)(2,1)}) custom-call(s32[32,6]{1,0:T(8,128)} %copy.17.lists_ref, s32[32]{0:T(128)} %counts_ref.1, bf16[32,128,128]{2,1,0:T(8,128)(2,1)} %copy-done.7, bf16[32,128,128]{2,1,0:T(8,128)(2,1)} %copy-done.8, bf16[64,128,256]{2,1,0:T(8,128)(2,1)} %copy-done), custom_call_target="tpu_custom_call" | custom-call | tf_op jit(solution)/shard_map/attend/pallas_call | solution.py:205
  138.0 0.0 copy-start.1
  138.0 2.2 %copy-done.1 = f32[32,128,256]{2,1,0:T(8,128)S(1)} copy-done((f32[32,128,256]{2,1,0:T(8,128)S(1)}, f32[32,128,256]{2,1,0:T(8,128)}, u32[]{:S(2)}) %copy-start.1) | copy-done | bytes 4194328
  140.2 0.0 copy-start.2
  140.2 1.6 copy-done.2
  141.7 1.2 copy-done.9
  143.0 67.5 %scatter.1 = (bf16[128,4096]{1,0:T(8,128)(2,1)S(1)}, bf16[128,4096]{1,0:T(8,128)(2,1)S(1)}, bf16[128,4096]{1,0:T(8,128)(2,1)S(1)}) custom-call(s32[64]{0:T(128)S(1)} %pad_add_fusion.named_ref, s32[64]{0:T(128)S(1)} %pad_add_fusion.1.rank_ref, bf16[32,128,128]{2,1,0:T(8,128)(2,1)S(1)} %copy-done.9, f32[32,128,256]{2,1,0:T(8,128)S(1)} %copy-done.1, ...), custom_call_target="tpu_custom_call" | custom-call | tf_op jit(solution)/shard_map/scatter/pallas_call | solution.py:290
  210.5 1.0 copy.21
  211.4 1.0 copy.22
  212.4 1.0 copy.23
  (7 shorter events, 0.0 us)
Async XLA Ops:
  0.6 6.0 %collective-permute-start.1 = (s32[32,6]{0,1:T(8,128)}, s32[32,6]{0,1:T(8,128)S(1)}, u32[]{:S(2)}, u32[]{:S(2)}) collective-permute-start(s32[32,6]{0,1:T(8,128)} %param.10), channel_id=1, source_target_pairs={{0,224},{32,0},{64,32},{96,64},{128,96},{160,128},{192,160},{224,1... | collective-permute-start | bytes 2312 | tf_op jit(solution)/shard_map/ppermute | solution.py:336
  3.9 4.9 %collective-permute-start = (s32[32,6]{0,1:T(8,128)}, s32[32,6]{0,1:T(8,128)S(1)}, u32[]{:S(2)}, u32[]{:S(2)}) collective-permute-start(s32[32,6]{0,1:T(8,128)} %param.10), channel_id=1, source_target_pairs={{0,32},{32,64},{64,96},{96,128},{128,160},{160,192},{192,224},{224... | collective-permute-start | bytes 2312 | tf_op jit(solution)/shard_map/ppermute | solution.py:335
  11.6 1.2 copy-start.3
  12.8 1.2 copy-start.4
  14.1 1.2 copy-start.5
  15.3 1.2 copy-start.6
  91.8 1.9 copy-start
  93.8 1.0 copy-start.7
  94.7 1.0 copy-start.8
  138.0 2.2 %copy-start.1 = (f32[32,128,256]{2,1,0:T(8,128)S(1)}, f32[32,128,256]{2,1,0:T(8,128)}, u32[]{:S(2)}) copy-start(f32[32,128,256]{2,1,0:T(8,128)} %get-tuple-element.13.own_ref) | copy-start | bytes 12582916
  140.2 1.6 copy-start.2
  141.7 1.2 copy-start.9

commit v2 on v0

v2 whole, which is shorter than its diff:
```python
import functools

import jax
import jax.numpy as jnp
from jax import lax
from jax.experimental import pallas as pl
from jax.experimental.pallas import tpu as pltpu
from jax.sharding import PartitionSpec as P

D = 128
NEAR = 16
MESH = pl.DeviceIdType.MESH
ANY = pl.BlockSpec(memory_space=pl.ANY)
VMEM = pl.BlockSpec(memory_space=pltpu.VMEM)
SCALE = D ** (-0.5)
LOG2E = 1.4426950408889634
GROUP = 4
STEPS = 8
PLACE, PAIR, QUERY, SAME, LAST, HAS, COUNT, NAMED, RANK, PICK = 0, 1, 2, 3, 4, 5, 6, 7, 9, 11


def peer_of(i, me, tiles):
    half = tiles // 2
    z, y, x = me // half, (me % half) // 4, me % 4
    z = (z + i) % 2
    x = (x + i // 2) % 4
    y = (y + i // 8) % (half // 4)
    return z * half + y * 4 + x


def greet(tiles, me, before, after):
    barrier = pltpu.get_barrier_semaphore()

    def hello(i, carry):
        pl.semaphore_signal(barrier, inc=1, device_id={"tile": peer_of(i, me, tiles)}, device_id_type=MESH)
        return carry

    lax.fori_loop(1, tiles, hello, 0)
    for frame in (before, after):
        pl.semaphore_signal(barrier, inc=1, device_id={"frame": frame}, device_id_type=MESH)
    pl.semaphore_wait(barrier, tiles + 1)


def wait_bytes(ref, sem):
    pltpu.make_async_copy(ref, ref, sem).wait()


def iota(shape, axis):
    return lax.broadcasted_iota(jnp.int32, shape, axis)


def add_up(x, axis):
    return jnp.sum(x, axis=axis, keepdims=True)


def down(row):
    return jnp.broadcast_to(row, (128, 128)).T


def naming(lists, slots, nblk):
    w = iota((nblk, 128), 1)
    hits = [(lists[:, s : s + 1] == w).astype(jnp.int32) for s in range(slots)]
    named = functools.reduce(jnp.maximum, hits)
    named = jnp.max(named, axis=0, keepdims=True)
    a, b = iota((128, 128), 0), iota((128, 128), 1)

    def group(x):
        return (x >= nblk).astype(jnp.int32) + (x >= 2 * nblk).astype(jnp.int32)

    rank = add_up(jnp.where((a < b) & (group(a) == group(b)), down(named), 0), 0)
    return hits, named, jnp.minimum(rank, NEAR - 1)


def own_table(lists, slots, nblk, table):
    hits, _, rank = naming(lists, slots, nblk)
    w = iota((1, 128), 1)
    place = jnp.where(w < nblk, nblk + rank, jnp.where(w < 2 * nblk, w - nblk, nblk + NEAR + rank))
    pairs = nblk * slots
    at = jnp.concatenate([add_up(hit * place, 1) for hit in hits], 0)
    at = jnp.broadcast_to(at, (pairs, 256))
    p, t = iota((pairs, 256), 0), iota((pairs, 256), 1)
    key = at * 256 + p
    padded = jnp.concatenate([key[:, :128], jnp.full((256 - pairs, 128), 1 << 20, jnp.int32)], 0)
    row = jnp.concatenate([padded[:128].T[0:1], padded[128:].T[0:1]], 1)
    order = add_up((row < key).astype(jnp.int32), 1)
    here, ahead = order == t, order + 1 == t
    sorted_place = add_up(jnp.where(here, at, 0), 0)
    place_before = add_up(jnp.where(ahead, at, 0), 0)
    first = iota((1, 256), 1) == 0
    r = iota((nblk, 256), 0)
    rows = {
        PLACE: add_up(jnp.where(p == t, at, 0), 0),
        PAIR: add_up(jnp.where(here, p, 0), 0),
        QUERY: add_up(jnp.where(here, p % nblk, 0), 0),
        SAME: jnp.where(first, 0, (sorted_place == place_before).astype(jnp.int32)),
        LAST: jnp.maximum(add_up((at <= t).astype(jnp.int32), 0) - 1, 0),
        HAS: add_up((at == t).astype(jnp.int32), 0),
        COUNT: add_up(jnp.where(r == iota((nblk, 256), 1), lists[:, slots : slots + 1], 0), 0),
    }
    for i, value in rows.items():
        table[i : i + 1, :] = value


def near_table(lists, slots, nblk, start, side, table):
    _, named, rank = naming(lists, slots, nblk)
    w, n = iota((128, 128), 0), iota((128, 128), 1)
    hit = (down(named) > 0) & (down(rank) == n) & (w >= start) & (w < start + nblk)
    table[NAMED + side : NAMED + side + 1, 0:128] = named
    table[RANK + side : RANK + side + 1, 0:128] = rank
    table[PICK + side : PICK + side + 1, 0:128] = add_up(jnp.where(hit, w - start, 0), 0)


def f32dot(a, b):
    return jnp.dot(a, b, preferred_element_type=jnp.float32)


def attend(rs, counts, places, slots, nblk, q_ref, g_ref, kv_ref, kt_ref, terms_ref, dq_ref):
    both, score, dprob, top, low = [], [], [], [], []
    for r in rs:
        q, g = q_ref[r], g_ref[r]
        zero = jnp.zeros_like(q)
        both.append(jnp.concatenate([jnp.concatenate([q, zero], 1), jnp.concatenate([zero, g], 1)], 0))
    for b, count, place in zip(both, counts, places):
        score.append([])
        dprob.append([])
        high = None
        for s in range(slots):
            out = lax.dot_general(
                kv_ref[place[s]], b, (((1,), (1,)), ((), ())), preferred_element_type=jnp.float32
            )
            x = out[:, :D] * (SCALE * LOG2E)
            if s >= 2:
                x = jnp.where(s < count, x, -1e30)
            score[-1].append(x)
            dprob[-1].append(out[:, D:])
            x = jnp.max(x, axis=0, keepdims=True)
            high = x if high is None else jnp.maximum(high, x)
        top.append(high)
    inverse = []
    for x, high in zip(score, top):
        total = 0.0
        for s in range(slots):
            x[s] = jnp.exp2(x[s] - high)
            total = total + jnp.sum(x[s], axis=0, keepdims=True)
        inverse.append(1.0 / total)
    for a, r in enumerate(rs):
        delta = 0.0
        for s in range(slots):
            score[a][s] = score[a][s] * inverse[a]
            low = score[a][s].astype(jnp.bfloat16)
            terms_ref[s * nblk + r, :, D : 2 * D] = low
            delta = delta + jnp.sum(low.astype(jnp.float32) * dprob[a][s], axis=0, keepdims=True)
        dlow = []
        for s in range(slots):
            dlow.append((score[a][s] * (dprob[a][s] - delta)).astype(jnp.bfloat16))
            terms_ref[s * nblk + r, :, 0:D] = dlow[s]
        dq = f32dot(
            jnp.concatenate([kt_ref[places[a][s]] for s in range(slots)], 1), jnp.concatenate(dlow, 0)
        )
        dq_ref[r] = (dq * SCALE).T.astype(jnp.bfloat16)


def kernel(tiles, frames, slots, lists_ref, q_in, k_in, v_in, g_in, dq_out, dk_out, dv_out,
           own, kv, packed, parts, q_ref, g_ref, kt, terms, sums, dq_ref, near_lists, table, scalars,
           send_sem, recv_sem, local_sem, near_send, near_recv):
    nblk = tiles
    pairs = nblk * slots
    me, frame = lax.axis_index("tile"), lax.axis_index("frame")
    before, after = (frame + frames - 1) % frames, (frame + 1) % frames
    mine = pl.ds(pl.multiple_of(me * D, D), D)
    greet(tiles, me, before, after)

    def to_neighbours(stage, sources, targets):
        copies = []
        for side, frame_to in ((0, before), (1, after)):
            copies.append(pltpu.make_async_remote_copy(
                src_ref=sources[side], dst_ref=targets[1 - side],
                send_sem=near_send.at[stage, side], recv_sem=near_recv.at[stage, side],
                device_id={"frame": frame_to}, device_id_type=MESH,
            ))
        return copies

    list_copies = to_neighbours(0, [lists_ref, lists_ref], [near_lists.at[0], near_lists.at[1]])
    for copy in list_copies:
        copy.start()
    lands = (
        lambda t: own.at[t, :, pl.ds(0, D)],
        lambda t: own.at[t, :, pl.ds(D, D)],
        lambda t: q_ref.at[t],
        lambda t: g_ref.at[t],
    )
    local = []
    for a, src in enumerate((k_in, v_in, q_in, g_in)):
        def send(i, carry, a=a, src=src):
            to = peer_of(i, me, tiles)
            pltpu.make_async_remote_copy(
                src_ref=src.at[:, pl.ds(pl.multiple_of(to * D, D), D)], dst_ref=lands[a](me),
                send_sem=send_sem.at[a], recv_sem=recv_sem.at[a],
                device_id={"tile": to}, device_id_type=MESH,
            ).start()
            return carry

        lax.fori_loop(1, tiles, send, 0)
        local.append(pltpu.make_async_copy(src.at[:, mine], lands[a](me), local_sem.at[a]))
        local[a].start()

    table[...] = jnp.zeros_like(table)
    own_table(lists_ref[...], slots, nblk, table)
    for copy in list_copies:
        copy.wait()
    near_table(near_lists[0], slots, nblk, 2 * nblk, 0, table)
    near_table(near_lists[1], slots, nblk, 0, 1, table)
    to_scalars = pltpu.make_async_copy(table, scalars, local_sem.at[4])
    to_scalars.start()
    to_scalars.wait()

    for a in range(2):
        wait_bytes(own.at[pl.ds(0, tiles - 1), :, pl.ds(0, D)], recv_sem.at[a])
        local[a].wait()
    for side in range(2):
        def pack(n, carry, side=side):
            packed[side, n] = own[scalars[PICK + side, n]]
            return carry

        lax.fori_loop(0, NEAR, pack, 0)
    kv_copies = to_neighbours(
        1, [packed.at[0], packed.at[1]], [kv.at[pl.ds(nblk, NEAR)], kv.at[pl.ds(nblk + NEAR, NEAR)]]
    )
    for copy in kv_copies:
        copy.start()
    keep = pltpu.make_async_copy(own, kv.at[pl.ds(0, nblk)], local_sem.at[4])
    keep.start()

    def turn_own(j, carry):
        kt[j] = own[j, :, 0:D].T
        return carry

    lax.fori_loop(0, nblk, turn_own, 0)
    for a in range(2, 4):
        wait_bytes(q_ref.at[pl.ds(0, tiles - 1)], recv_sem.at[a])
        local[a].wait()
    keep.wait()
    for copy in kv_copies:
        copy.wait()

    def turn_near(j, carry):
        kt[nblk + j] = kv[nblk + j, :, 0:D].T
        return carry

    lax.fori_loop(0, 2 * NEAR, turn_near, 0)

    def blocks(i, carry):
        rs = [peer_of(i * GROUP + a, me, tiles) for a in range(GROUP)]
        attend(
            rs, [scalars[COUNT, r] for r in rs],
            [[scalars[PLACE, s * nblk + r] for s in range(slots)] for r in rs],
            slots, nblk, q_ref, g_ref, kv, kt, terms, dq_ref,
        )
        for a, r in enumerate(rs):
            @pl.when(i * GROUP + a > 0)
            def _(r=r):
                pltpu.make_async_remote_copy(
                    src_ref=dq_ref.at[r], dst_ref=dq_out.at[:, mine],
                    send_sem=send_sem.at[4], recv_sem=recv_sem.at[4],
                    device_id={"tile": r}, device_id_type=MESH,
                ).start()
        return carry

    lax.fori_loop(0, nblk // GROUP, blocks, 0)
    finals = [pltpu.make_async_copy(dq_ref.at[me], dq_out.at[:, mine], local_sem.at[5])]
    finals[0].start()

    def add(i, total):
        for u in range(STEPS):
            t = i * STEPS + u
            term = terms[scalars[PAIR, t]]
            r = scalars[QUERY, t]
            term = jnp.concatenate([f32dot(term[:, :D], q_ref[r]), f32dot(term[:, D:], g_ref[r])], 1)
            total = jnp.where(scalars[SAME, t] > 0, total, 0.0) + term
            sums[t] = total
        return total

    lax.fori_loop(0, pairs // STEPS, add, jnp.zeros((D, 2 * D), jnp.float32))

    def summed(j):
        total = jnp.where(scalars[HAS, j] > 0, sums[scalars[LAST, j]], 0.0)
        return jnp.concatenate([total[:, :D] * SCALE, total[:, D:]], 1)

    for side in range(2):
        def part(n, carry, side=side):
            packed[side, n] = summed(nblk + side * NEAR + n).astype(jnp.bfloat16)
            return carry

        lax.fori_loop(0, NEAR, part, 0)
    part_copies = to_neighbours(2, [packed.at[0], packed.at[1]], [parts.at[0], parts.at[1]])
    for copy in part_copies:
        copy.start()
    for copy in part_copies:
        copy.wait()

    def settle(to):
        total = summed(to)
        for side, start in ((0, 2 * nblk), (1, 0)):
            named, rank = scalars[NAMED + side, start + to], scalars[RANK + side, start + to]
            total = total + jnp.where(named > 0, parts[side, rank].astype(jnp.float32), 0.0)
        own[to] = total.astype(jnp.bfloat16)

    def send_back(i, carry):
        to = peer_of(i, me, tiles)
        settle(to)
        for a, out in ((0, dk_out), (1, dv_out)):
            pltpu.make_async_remote_copy(
                src_ref=own.at[to, :, pl.ds(a * D, D)], dst_ref=out.at[:, mine],
                send_sem=send_sem.at[5 + a], recv_sem=recv_sem.at[5 + a],
                device_id={"tile": to}, device_id_type=MESH,
            ).start()
        return carry

    lax.fori_loop(1, tiles, send_back, 0)
    settle(me)
    for a, out in ((0, dk_out), (1, dv_out)):
        copy = pltpu.make_async_copy(own.at[me, :, pl.ds(a * D, D)], out.at[:, mine], local_sem.at[6 + a])
        copy.start()
        finals.append(copy)
    for copy in finals:
        copy.wait()
    for a in range(7):
        wait_bytes(q_ref.at[pl.ds(0, tiles - 1)], send_sem.at[a])
    for a in range(4, 7):
        wait_bytes(q_ref.at[pl.ds(0, tiles - 1)], recv_sem.at[a])


def local(tiles, frames, queries, keys, values, out_grad, key_lists, key_counts):
    nblk, slots = key_lists.shape
    bf16, f32, i32 = jnp.bfloat16, jnp.float32, jnp.int32
    lists = jnp.concatenate([key_lists, key_counts[:, None]], 1)
    lists = jnp.pad(lists, ((0, 0), (0, 128 - slots - 1)), constant_values=-1)
    out = jax.ShapeDtypeStruct((D, tiles * D), bf16)
    return pl.pallas_call(
        functools.partial(kernel, tiles, frames, slots),
        out_shape=(out, out, out),
        in_specs=[VMEM, ANY, ANY, ANY, ANY],
        out_specs=(ANY, ANY, ANY),
        scratch_shapes=[
            pltpu.VMEM((nblk, D, 2 * D), bf16),
            pltpu.VMEM((nblk + 2 * NEAR, D, 2 * D), bf16),
            pltpu.VMEM((2, NEAR, D, 2 * D), bf16),
            pltpu.VMEM((2, NEAR, D, 2 * D), bf16),
            pltpu.VMEM((nblk, D, D), bf16),
            pltpu.VMEM((nblk, D, D), bf16),
            pltpu.VMEM((nblk + 2 * NEAR, D, D), bf16),
            pltpu.VMEM((nblk * slots, D, 2 * D), bf16),
            pltpu.VMEM((nblk * slots, D, 2 * D), f32),
            pltpu.VMEM((nblk, D, D), bf16),
            pltpu.VMEM((2, nblk, 128), i32),
            pltpu.VMEM((16, 256), i32),
            pltpu.SMEM((16, 256), i32),
            pltpu.SemaphoreType.DMA((7,)),
            pltpu.SemaphoreType.DMA((7,)),
            pltpu.SemaphoreType.DMA((8,)),
            pltpu.SemaphoreType.DMA((3, 2)),
            pltpu.SemaphoreType.DMA((3, 2)),
        ],
        compiler_params=pltpu.CompilerParams(
            collective_id=0, has_side_effects=True, vmem_limit_bytes=60 * 2**20
        ),
        name="backward",
    )(lists, queries, keys, values, out_grad)


def solution(mesh):
    both = P(("frame", "tile"), None)
    return jax.shard_map(
        functools.partial(local, mesh.shape["tile"], mesh.shape["frame"]),
        mesh=mesh,
        in_specs=(both, both, both, both, P("frame", None), P("frame")),
        out_specs=(both, both, both),
        check_vma=False,
    )
```

time: 419 us -> 170 us (0.41); the launches traced: 414 us -> 170 us
  Pallas kernels: 0 us -> 162 us
  waiting for transfers between devices: 105 us -> 0 us
  other arithmetic: 99.6 us -> 0.69 us
  starting transfers between devices: 96.4 us -> 0 us
  matrix products: 53.5 us -> 0 us
  local copies, waits for them, and re-layouts: 58.6 us -> 6.3 us
    pallas_call x0 -> x1, Pallas kernels: none -> 162 us  [local(): pl.pallas_call(functools.partial(kernel, tiles, frames, slots), out_shape...]
    scatter-add x2 -> x0, other arithmetic: 79.3 us -> none  [the longest x1 39.7 us: attend_back(): dv = jnp.zeros(k_all.shape, jnp.float32).at[lists].add(value_terms)]
    all_to_all x7 -> x0, starting transfers between devices: 73.3 us -> none  [the longest x1 22.4 us: local(): lax.all_to_all(out_grad, 'tile', split_axis=1, concat_axis=0, tiled=True)]
    ppermute x8 -> x0, waiting for transfers between devices: 60.3 us -> none  [shifted(): return lax.ppermute(array, axis, pairs)]
    dot_general x6 -> x0, matrix products: 53.5 us -> none  [the longest x1 11.4 us: attend_back(): jnp.einsum('nhasb,nahd->nsbhd', plow, g_blocks, preferred_element_type=jn...]
    all_to_all x7 -> x0, waiting for transfers between devices: 44.9 us -> none  [the longest x1 12.8 us: local(): lax.all_to_all(keys, 'tile', split_axis=1, concat_axis=0, tiled=True)]
    gather x4 -> x0, local copies, waits for them, and re-layouts: 33.5 us -> none  [the longest x2 16.8 us: attend_back(): k_listed = jnp.take(k_all, lists, axis=0)]
    ppermute x8 -> x0, starting transfers between devices: 23.1 us -> none  [shifted(): return lax.ppermute(array, axis, pairs)]
  transfers between devices with their start and end apart: 15 -> 0, of which waited for: 10 -> 0; matrix products, arithmetic and copies ran while one was open for 43% -> 0% of each run, Pallas kernels for 0% -> 0%
where the time goes in v2:
time: 170 us
  Pallas kernels  162 us (95%)
  local copies, waits for them, and re-layouts  6.3 us (4%)
    pallas_call x1, Pallas kernels, local(): pl.pallas_call(functools.partial(kernel, tiles, frames, slots), out_shape...  162 us
    unnamed x9, local copies, waits for them, and re-layouts  5.6 us

profile of v2, /device:TPU:1, one launch (start us, length us, event | category | flops | bytes accessed | tf_op | source)
XLA Modules:
  0.0 169.6 jit_solution(523819740730135549)
XLA Ops:
  0.6 0.0 copy-start.2
  0.6 0.6 copy-done.2
  1.3 0.7 pad_add_fusion
  2.0 0.1 copy.11
  2.1 0.6 pad.4.lists_ref
  2.7 162.0 %backward.1 = (bf16[128,4096]{1,0:T(8,128)(2,1)}, bf16[128,4096]{1,0:T(8,128)(2,1)}, bf16[128,4096]{1,0:T(8,128)(2,1)}) custom-call(s32[32,128]{1,0:T(8,128)} %pad.4.lists_ref, bf16[128,4096]{1,0:T(8,128)(2,1)} %q_in.1, bf16[128,4096]{1,0:T(8,128)(2,1)} %k_in.1, bf16[128,4096]{1,0:T(8,128)(2,1)} %v_in.1, bf16[128,4096]{1,0:T(8,128)(2,1)} %g_in.1), custom_call_target="tpu_custom_call" | custom-call | tf_op jit(solution)/shard_map/backward/pallas_call | solution.py:339
  164.7 0.0 copy-start.1
  164.7 2.4 %copy.15 = bf16[128,4096]{1,0:T(8,128)(2,1)} copy(bf16[128,4096]{1,0:T(8,128)(2,1)} %get-tuple-element.6) | data formatting | bytes 2097152
  167.1 0.0 copy-done.1
  167.1 0.0 copy-start
  167.1 1.0 copy.16
  168.0 0.6 copy-done
  168.7 1.0 copy.17
Async XLA Ops:
  0.6 0.7 copy-start.2
  164.7 2.4 %copy-start.1 = (bf16[128,4096]{1,0:T(8,128)(2,1)S(1)}, bf16[128,4096]{1,0:T(8,128)(2,1)}, u32[]{:S(2)}) copy-start(bf16[128,4096]{1,0:T(8,128)(2,1)} %get-tuple-element.7) | copy-start | bytes 3145732
  167.1 1.6 copy-start

commit v3 on v2

--- a/solution.py
+++ b/solution.py
@@ -21,11 +21,28 @@
 
 def peer_of(i, me, tiles):
     half = tiles // 2
-    z, y, x = me // half, (me % half) // 4, me % 4
-    z = (z + i) % 2
-    x = (x + i // 2) % 4
-    y = (y + i // 8) % (half // 4)
+    z, y, x = lax.div(me, half), lax.div(lax.rem(me, half), 4), lax.rem(me, 4)
+    z = lax.rem(z + i, 2)
+    x = lax.rem(x + lax.div(i, 2), 4)
+    y = lax.rem(y + lax.div(i, 8), half // 4)
     return z * half + y * 4 + x
+
+
+def sender_of(i, me, tiles):
+    half = tiles // 2
+    z, y, x = lax.div(me, half), lax.div(lax.rem(me, half), 4), lax.rem(me, 4)
+    z = lax.rem(z + i, 2)
+    x = lax.rem(x + 4 - lax.rem(lax.div(i, 2), 4), 4)
+    y = lax.rem(y + half // 4 - lax.div(i, 8), half // 4)
+    return z * half + y * 4 + x
+
+
+def near_first(k, tiles):
+    return lax.rem(2 * k, tiles) + lax.div(k, tiles // 2)
+
+
+def far_first(k, tiles):
+    return 2 * k - 1 - lax.div(k, tiles // 2 + 1) * (tiles - 1)
 
 
 def greet(tiles, me, before, after):
@@ -55,6 +72,11 @@
 
 def down(row):
     return jnp.broadcast_to(row, (128, 128)).T
+
+
+def turned(lists, nblk):
+    rest = jnp.zeros((128 - lists.shape[0], 128), jnp.int32)
+    return jnp.concatenate([lists, rest], 0).T[:nblk]
 
 
 def naming(lists, slots, nblk):
@@ -87,7 +109,6 @@
     sorted_place = add_up(jnp.where(here, at, 0), 0)
     place_before = add_up(jnp.where(ahead, at, 0), 0)
     first = iota((1, 256), 1) == 0
-    r = iota((nblk, 256), 0)
     rows = {
         PLACE: add_up(jnp.where(p == t, at, 0), 0),
         PAIR: add_up(jnp.where(here, p, 0), 0),
@@ -95,7 +116,6 @@
         SAME: jnp.where(first, 0, (sorted_place == place_before).astype(jnp.int32)),
         LAST: jnp.maximum(add_up((at <= t).astype(jnp.int32), 0) - 1, 0),
         HAS: add_up((at == t).astype(jnp.int32), 0),
-        COUNT: add_up(jnp.where(r == iota((nblk, 256), 1), lists[:, slots : slots + 1], 0), 0),
     }
     for i, value in rows.items():
         table[i : i + 1, :] = value
@@ -160,14 +180,20 @@
         dq_ref[r] = (dq * SCALE).T.astype(jnp.bfloat16)
 
 
-def kernel(tiles, frames, slots, lists_ref, q_in, k_in, v_in, g_in, dq_out, dk_out, dv_out,
-           own, kv, packed, parts, q_ref, g_ref, kt, terms, sums, dq_ref, near_lists, table, scalars,
-           send_sem, recv_sem, local_sem, near_send, near_recv):
+def kernel(tiles, frames, slots, lists_in, counts_in, q_in, k_in, v_in, g_in, dq_out, dk_out, dv_out,
+           own_k, own_v, kv, packed, parts_k, parts_v, q_ref, g_ref, kt, terms, sums, dq_ref, own_lists, counts, lists_ref, near_lists, table, scalars,
+           send_sem, recv_sem, qg_sem, local_sem, near_send, near_recv):
     nblk = tiles
     pairs = nblk * slots
     me, frame = lax.axis_index("tile"), lax.axis_index("frame")
-    before, after = (frame + frames - 1) % frames, (frame + 1) % frames
+    before, after = lax.rem(frame + frames - 1, frames), lax.rem(frame + 1, frames)
     mine = pl.ds(pl.multiple_of(me * D, D), D)
+    loads = [
+        pltpu.make_async_copy(lists_in, own_lists, local_sem.at[4]),
+        pltpu.make_async_copy(counts_in, counts, local_sem.at[5]),
+    ]
+    for copy in loads:
+        copy.start()
     greet(tiles, me, before, after)
 
     def to_neighbours(stage, sources, targets):
@@ -180,67 +206,95 @@
             ))
         return copies
 
+    def gather(src, place, start, stop, sent, arrived):
+        def send(i, carry):
+            to = peer_of(i, me, tiles)
+            pltpu.make_async_remote_copy(
+                src_ref=src.at[:, pl.ds(pl.multiple_of(to * D, D), D)], dst_ref=place(me),
+                send_sem=sent, recv_sem=arrived(i),
+                device_id={"tile": to}, device_id_type=MESH,
+            ).start()
+            return carry
+
+        lax.fori_loop(start, stop, send, 0)
+
+    def keep_own(src, place, sem):
+        copy = pltpu.make_async_copy(src.at[:, mine], place(me), sem)
+        copy.start()
+        return copy
+
+    own = (own_k, own_v)
+    kv_land = (lambda t: own_k.at[t], lambda t: own_v.at[t])
+    qg_land = (lambda t: q_ref.at[t], lambda t: g_ref.at[t])
+    local = []
+    for a, src in enumerate((k_in, v_in)):
+        gather(src, kv_land[a], 1, tiles, send_sem.at[a], lambda i: recv_sem.at[a])
+        local.append(keep_own(src, kv_land[a], local_sem.at[a]))
+
+    def gather_qg(start, stop):
+        def send(i, carry):
+            i = near_first(i, tiles)
+            to = peer_of(i, me, tiles)
+            for a, src in enumerate((q_in, g_in)):
+                pltpu.make_async_remote_copy(
+                    src_ref=src.at[:, pl.ds(pl.multiple_of(to * D, D), D)], dst_ref=qg_land[a](me),
+                    send_sem=send_sem.at[2 + a], recv_sem=qg_sem.at[a, i],
+                    device_id={"tile": to}, device_id_type=MESH,
+                ).start()
+            return carry
+
+        lax.fori_loop(start, stop, send, 0)
+
+    for a, src in enumerate((q_in, g_in)):
+        local.append(keep_own(src, qg_land[a], qg_sem.at[a, 0]))
+    gather_qg(1, tiles // 2)
+
+    for copy in loads:
+        copy.wait()
+    lists_ref[...] = jnp.zeros_like(lists_ref)
+    lists_ref[0:slots, 0:nblk] = own_lists[...]
     list_copies = to_neighbours(0, [lists_ref, lists_ref], [near_lists.at[0], near_lists.at[1]])
     for copy in list_copies:
         copy.start()
-    lands = (
-        lambda t: own.at[t, :, pl.ds(0, D)],
-        lambda t: own.at[t, :, pl.ds(D, D)],
-        lambda t: q_ref.at[t],
-        lambda t: g_ref.at[t],
-    )
-    local = []
-    for a, src in enumerate((k_in, v_in, q_in, g_in)):
-        def send(i, carry, a=a, src=src):
-            to = peer_of(i, me, tiles)
-            pltpu.make_async_remote_copy(
-                src_ref=src.at[:, pl.ds(pl.multiple_of(to * D, D), D)], dst_ref=lands[a](me),
-                send_sem=send_sem.at[a], recv_sem=recv_sem.at[a],
-                device_id={"tile": to}, device_id_type=MESH,
-            ).start()
-            return carry
-
-        lax.fori_loop(1, tiles, send, 0)
-        local.append(pltpu.make_async_copy(src.at[:, mine], lands[a](me), local_sem.at[a]))
-        local[a].start()
 
     table[...] = jnp.zeros_like(table)
-    own_table(lists_ref[...], slots, nblk, table)
+    table[COUNT : COUNT + 1, 0:nblk] = counts[...]
+    own_table(turned(lists_ref[...], nblk), slots, nblk, table)
     for copy in list_copies:
         copy.wait()
-    near_table(near_lists[0], slots, nblk, 2 * nblk, 0, table)
-    near_table(near_lists[1], slots, nblk, 0, 1, table)
+    near_table(turned(near_lists[0], nblk), slots, nblk, 2 * nblk, 0, table)
+    near_table(turned(near_lists[1], nblk), slots, nblk, 0, 1, table)
     to_scalars = pltpu.make_async_copy(table, scalars, local_sem.at[4])
     to_scalars.start()
     to_scalars.wait()
 
+    keep, kv_copies = [], []
     for a in range(2):
-        wait_bytes(own.at[pl.ds(0, tiles - 1), :, pl.ds(0, D)], recv_sem.at[a])
+        wait_bytes(own[a].at[pl.ds(0, tiles - 1)], recv_sem.at[a])
         local[a].wait()
-    for side in range(2):
-        def pack(n, carry, side=side):
-            packed[side, n] = own[scalars[PICK + side, n]]
-            return carry
-
-        lax.fori_loop(0, NEAR, pack, 0)
-    kv_copies = to_neighbours(
-        1, [packed.at[0], packed.at[1]], [kv.at[pl.ds(nblk, NEAR)], kv.at[pl.ds(nblk + NEAR, NEAR)]]
-    )
-    for copy in kv_copies:
-        copy.start()
-    keep = pltpu.make_async_copy(own, kv.at[pl.ds(0, nblk)], local_sem.at[4])
-    keep.start()
+        for side in range(2):
+            def pack(n, carry, a=a, side=side):
+                packed[a, side, n] = own[a][scalars[PICK + side, n]]
+                return carry
+
+            lax.fori_loop(0, NEAR, pack, 0)
+        cut = pl.ds(a * D, D)
+        kv_copies += to_neighbours(
+            1 + a, [packed.at[a, 0], packed.at[a, 1]],
+            [kv.at[pl.ds(nblk, NEAR), :, cut], kv.at[pl.ds(nblk + NEAR, NEAR), :, cut]],
+        )
+        for copy in kv_copies[-2:]:
+            copy.start()
+        keep.append(pltpu.make_async_copy(own[a], kv.at[pl.ds(0, nblk), :, cut], local_sem.at[4 + a]))
+        keep[a].start()
+    gather_qg(tiles // 2, tiles)
 
     def turn_own(j, carry):
-        kt[j] = own[j, :, 0:D].T
+        kt[j] = own_k[j].T
         return carry
 
     lax.fori_loop(0, nblk, turn_own, 0)
-    for a in range(2, 4):
-        wait_bytes(q_ref.at[pl.ds(0, tiles - 1)], recv_sem.at[a])
-        local[a].wait()
-    keep.wait()
-    for copy in kv_copies:
+    for copy in keep + kv_copies:
         copy.wait()
 
     def turn_near(j, carry):
@@ -250,24 +304,31 @@
     lax.fori_loop(0, 2 * NEAR, turn_near, 0)
 
     def blocks(i, carry):
-        rs = [peer_of(i * GROUP + a, me, tiles) for a in range(GROUP)]
+        steps = [near_first(i * GROUP + a, tiles) for a in range(GROUP)]
+        rs = [sender_of(step, me, tiles) for step in steps]
+        for a, r in enumerate(rs):
+            for b, place in enumerate(qg_land):
+                wait_bytes(place(r), qg_sem.at[b, steps[a]])
         attend(
             rs, [scalars[COUNT, r] for r in rs],
             [[scalars[PLACE, s * nblk + r] for s in range(slots)] for r in rs],
             slots, nblk, q_ref, g_ref, kv, kt, terms, dq_ref,
         )
-        for a, r in enumerate(rs):
-            @pl.when(i * GROUP + a > 0)
-            def _(r=r):
-                pltpu.make_async_remote_copy(
-                    src_ref=dq_ref.at[r], dst_ref=dq_out.at[:, mine],
-                    send_sem=send_sem.at[4], recv_sem=recv_sem.at[4],
-                    device_id={"tile": r}, device_id_type=MESH,
-                ).start()
         return carry
 
     lax.fori_loop(0, nblk // GROUP, blocks, 0)
-    finals = [pltpu.make_async_copy(dq_ref.at[me], dq_out.at[:, mine], local_sem.at[5])]
+
+    def send_dq(i, carry):
+        to = peer_of(far_first(i, tiles), me, tiles)
+        pltpu.make_async_remote_copy(
+            src_ref=dq_ref.at[to], dst_ref=dq_out.at[:, mine],
+            send_sem=send_sem.at[4], recv_sem=recv_sem.at[4],
+            device_id={"tile": to}, device_id_type=MESH,
+        ).start()
+        return carry
+
+    lax.fori_loop(1, tiles, send_dq, 0)
+    finals = [pltpu.make_async_copy(dq_ref.at[me], dq_out.at[:, mine], local_sem.at[0])]
     finals[0].start()
 
     def add(i, total):
@@ -282,44 +343,53 @@
 
     lax.fori_loop(0, pairs // STEPS, add, jnp.zeros((D, 2 * D), jnp.float32))
 
-    def summed(j):
-        total = jnp.where(scalars[HAS, j] > 0, sums[scalars[LAST, j]], 0.0)
-        return jnp.concatenate([total[:, :D] * SCALE, total[:, D:]], 1)
-
-    for side in range(2):
-        def part(n, carry, side=side):
-            packed[side, n] = summed(nblk + side * NEAR + n).astype(jnp.bfloat16)
-            return carry
-
-        lax.fori_loop(0, NEAR, part, 0)
-    part_copies = to_neighbours(2, [packed.at[0], packed.at[1]], [parts.at[0], parts.at[1]])
-    for copy in part_copies:
-        copy.start()
-    for copy in part_copies:
-        copy.wait()
-
-    def settle(to):
-        total = summed(to)
-        for side, start in ((0, 2 * nblk), (1, 0)):
-            named, rank = scalars[NAMED + side, start + to], scalars[RANK + side, start + to]
-            total = total + jnp.where(named > 0, parts[side, rank].astype(jnp.float32), 0.0)
-        own[to] = total.astype(jnp.bfloat16)
-
-    def send_back(i, carry):
-        to = peer_of(i, me, tiles)
-        settle(to)
-        for a, out in ((0, dk_out), (1, dv_out)):
+    parts = (parts_k, parts_v)
+    part_copies = []
+    for a in (1, 0):
+        cut = pl.ds(a * D, D)
+        for side in range(2):
+            def part(n, carry, a=a, side=side, cut=cut):
+                j = nblk + side * NEAR + n
+                total = jnp.where(scalars[HAS, j] > 0, sums[scalars[LAST, j], :, cut], 0.0)
+                if a == 0:
+                    total = total * SCALE
+                packed[a, side, n] = total.astype(jnp.bfloat16)
+                return carry
+
+            lax.fori_loop(0, NEAR, part, 0)
+        part_copies.append(to_neighbours(
+            3 + a, [packed.at[a, side] for side in range(2)], [parts[a].at[side] for side in range(2)]
+        ))
+        for copy in part_copies[-1]:
+            copy.start()
+
+    for a, out, copies in ((1, dv_out, part_copies[0]), (0, dk_out, part_copies[1])):
+        cut = pl.ds(a * D, D)
+        for copy in copies:
+            copy.wait()
+
+        def settle(to, cut=cut, a=a):
+            total = jnp.where(scalars[HAS, to] > 0, sums[scalars[LAST, to], :, cut], 0.0)
+            if a == 0:
+                total = total * SCALE
+            for side, start in ((0, 2 * nblk), (1, 0)):
+                named, rank = scalars[NAMED + side, start + to], scalars[RANK + side, start + to]
+                total = total + jnp.where(named > 0, parts[a][side, rank].astype(jnp.float32), 0.0)
+            own[a][to] = total.astype(jnp.bfloat16)
+
+        def send_back(i, carry, a=a, out=out, settle=settle):
+            to = peer_of((far_first, near_first)[a](i, tiles), me, tiles)
+            settle(to)
             pltpu.make_async_remote_copy(
-                src_ref=own.at[to, :, pl.ds(a * D, D)], dst_ref=out.at[:, mine],
+                src_ref=own[a].at[to], dst_ref=out.at[:, mine],
                 send_sem=send_sem.at[5 + a], recv_sem=recv_sem.at[5 + a],
                 device_id={"tile": to}, device_id_type=MESH,
             ).start()
-        return carry
-
-    lax.fori_loop(1, tiles, send_back, 0)
-    settle(me)
-    for a, out in ((0, dk_out), (1, dv_out)):
-        copy = pltpu.make_async_copy(own.at[me, :, pl.ds(a * D, D)], out.at[:, mine], local_sem.at[6 + a])
+            return carry
+
+        lax.fori_loop(1, tiles, send_back, 0)
+        settle(me)
+        copy = pltpu.make_async_copy(own[a].at[me], out.at[:, mine], local_sem.at[1 + a])
         copy.start()
         finals.append(copy)
     for copy in finals:
@@ -330,42 +400,63 @@
         wait_bytes(q_ref.at[pl.ds(0, tiles - 1)], recv_sem.at[a])
 
 
+def hand_over(a_in, b_in, c_in, a_out, b_out, c_out, sem):
+    copies = []
+    for i, (src, dst) in enumerate(((a_in, a_out), (b_in, b_out), (c_in, c_out))):
+        copies.append(pltpu.make_async_copy(src, dst, sem.at[i]))
+        copies[-1].start()
+    for copy in copies:
+        copy.wait()
+
+
 def local(tiles, frames, queries, keys, values, out_grad, key_lists, key_counts):
     nblk, slots = key_lists.shape
     bf16, f32, i32 = jnp.bfloat16, jnp.float32, jnp.int32
-    lists = jnp.concatenate([key_lists, key_counts[:, None]], 1)
-    lists = jnp.pad(lists, ((0, 0), (0, 128 - slots - 1)), constant_values=-1)
     out = jax.ShapeDtypeStruct((D, tiles * D), bf16)
-    return pl.pallas_call(
+    grads = pl.pallas_call(
         functools.partial(kernel, tiles, frames, slots),
         out_shape=(out, out, out),
-        in_specs=[VMEM, ANY, ANY, ANY, ANY],
+        in_specs=[ANY] * 6,
         out_specs=(ANY, ANY, ANY),
         scratch_shapes=[
-            pltpu.VMEM((nblk, D, 2 * D), bf16),
+            pltpu.VMEM((nblk, D, D), bf16),
+            pltpu.VMEM((nblk, D, D), bf16),
             pltpu.VMEM((nblk + 2 * NEAR, D, 2 * D), bf16),
-            pltpu.VMEM((2, NEAR, D, 2 * D), bf16),
-            pltpu.VMEM((2, NEAR, D, 2 * D), bf16),
+            pltpu.VMEM((2, 2, NEAR, D, D), bf16),
+            pltpu.VMEM((2, NEAR, D, D), bf16),
+            pltpu.VMEM((2, NEAR, D, D), bf16),
             pltpu.VMEM((nblk, D, D), bf16),
             pltpu.VMEM((nblk, D, D), bf16),
             pltpu.VMEM((nblk + 2 * NEAR, D, D), bf16),
             pltpu.VMEM((nblk * slots, D, 2 * D), bf16),
             pltpu.VMEM((nblk * slots, D, 2 * D), f32),
             pltpu.VMEM((nblk, D, D), bf16),
-            pltpu.VMEM((2, nblk, 128), i32),
+            pltpu.VMEM((slots, nblk), i32),
+            pltpu.VMEM((1, nblk), i32),
+            pltpu.VMEM((8, 128), i32),
+            pltpu.VMEM((2, 8, 128), i32),
             pltpu.VMEM((16, 256), i32),
             pltpu.SMEM((16, 256), i32),
             pltpu.SemaphoreType.DMA((7,)),
             pltpu.SemaphoreType.DMA((7,)),
-            pltpu.SemaphoreType.DMA((8,)),
-            pltpu.SemaphoreType.DMA((3, 2)),
-            pltpu.SemaphoreType.DMA((3, 2)),
+            pltpu.SemaphoreType.DMA((2, nblk)),
+            pltpu.SemaphoreType.DMA((6,)),
+            pltpu.SemaphoreType.DMA((5, 2)),
+            pltpu.SemaphoreType.DMA((5, 2)),
         ],
         compiler_params=pltpu.CompilerParams(
             collective_id=0, has_side_effects=True, vmem_limit_bytes=60 * 2**20
         ),
         name="backward",
-    )(lists, queries, keys, values, out_grad)
+    )(key_lists.T, key_counts[None, :], queries, keys, values, out_grad)
+    return pl.pallas_call(
+        hand_over,
+        out_shape=(out, out, out),
+        in_specs=[VMEM] * 3,
+        out_specs=(ANY, ANY, ANY),
+        scratch_shapes=[pltpu.SemaphoreType.DMA((3,))],
+        name="hand_over",
+    )(*grads)
 
 
 def solution(mesh):

time: 170 us -> 150 us (0.88)
  Pallas kernels: 162 us -> 149 us
  local copies, waits for them, and re-layouts: 6.3 us -> 0 us
    pallas_call x1, Pallas kernels: 162 us -> 146 us  [local(): pl.pallas_call(functools.partial(kernel, tiles, frames, slots), out_shape...]
    unnamed x9 -> x0, local copies, waits for them, and re-layouts: 5.6 us -> none
    pallas_call x0 -> x1, Pallas kernels: none -> 3.54 us  [local(): pl.pallas_call(hand_over, out_shape=(out, out, out), in_specs=[VMEM] * 3,...]
where the time goes in v3:
time: 150 us
  Pallas kernels  149 us (99%)
    pallas_call x1, Pallas kernels, local(): pl.pallas_call(functools.partial(kernel, tiles, frames, slots), out_shape...  146 us
    pallas_call x1, Pallas kernels, local(): pl.pallas_call(hand_over, out_shape=(out, out, out), in_specs=[VMEM] * 3,...  3.54 us

profile of v3, /device:TPU:1, one launch (start us, length us, event | category | flops | bytes accessed | tf_op | source)
XLA Modules:
  0.0 150.1 jit_solution(15700721936861702314)
XLA Ops:
  0.6 145.9 %backward.1 = (bf16[128,4096]{1,0:T(8,128)(2,1)}, bf16[128,4096]{1,0:T(8,128)(2,1)}, bf16[128,4096]{1,0:T(8,128)(2,1)}) custom-call(s32[6,32]{1,0:T(8,128)} %bitcast.2, s32[1,32]{1,0:T(1,128)} %bitcast.3, bf16[128,4096]{1,0:T(8,128)(2,1)} %q_in.1, bf16[128,4096]{1,0:T(8,128)(2,1)} %k_in.1, bf16[128,4096]{1,0:T(8,128)(2,1)} %v_in.1, bf16[128,4096]{1,0:T(8,128)(2,1)} %g_in.1), custom_call_target="tpu_custom_call" | custom-call | tf_op jit(solution)/shard_map/backward/pallas_call | solution.py:416
  146.5 3.5 %hand_over.1 = (bf16[128,4096]{1,0:T(8,128)(2,1)}, bf16[128,4096]{1,0:T(8,128)(2,1)}, bf16[128,4096]{1,0:T(8,128)(2,1)}) custom-call(bf16[128,4096]{1,0:T(8,128)(2,1)} %get-tuple-element.6.a_in, bf16[128,4096]{1,0:T(8,128)(2,1)} %get-tuple-element.7.b_in, bf16[128,4096]{1,0:T(8,128)(2,1)} %get-tuple-element.8.c_in), custom_call_target="tpu_custom_call" | custom-call | tf_op jit(solution)/shard_map/hand_over/pallas_call | solution.py:452

commit v4 on v3

--- a/solution.py
+++ b/solution.py
@@ -11,11 +11,10 @@
 NEAR = 16
 MESH = pl.DeviceIdType.MESH
 ANY = pl.BlockSpec(memory_space=pl.ANY)
-VMEM = pl.BlockSpec(memory_space=pltpu.VMEM)
 SCALE = D ** (-0.5)
 LOG2E = 1.4426950408889634
 GROUP = 4
-STEPS = 8
+STEPS = 16
 PLACE, PAIR, QUERY, SAME, LAST, HAS, COUNT, NAMED, RANK, PICK = 0, 1, 2, 3, 4, 5, 6, 7, 9, 11
 
 
@@ -181,8 +180,8 @@
 
 
 def kernel(tiles, frames, slots, lists_in, counts_in, q_in, k_in, v_in, g_in, dq_out, dk_out, dv_out,
-           own_k, own_v, kv, packed, parts_k, parts_v, q_ref, g_ref, kt, terms, sums, dq_ref, own_lists, counts, lists_ref, near_lists, table, scalars,
-           send_sem, recv_sem, qg_sem, local_sem, near_send, near_recv):
+           own_k, own_v, kv, packed, parts_k, parts_v, q_ref, g_ref, kt, terms, sums, dq_ref, own_lists, counts, lists_ref, near_lists, table, scalars, staged,
+           send_sem, recv_sem, qg_sem, stage_sem, local_sem, near_send, near_recv):
     nblk = tiles
     pairs = nblk * slots
     me, frame = lax.axis_index("tile"), lax.axis_index("frame")
@@ -194,6 +193,10 @@
     ]
     for copy in loads:
         copy.start()
+    stage = []
+    for a, src in enumerate((k_in, v_in, q_in, g_in)):
+        stage.append(pltpu.make_async_copy(src, staged.at[a], stage_sem.at[a]))
+        stage[a].start()
     greet(tiles, me, before, after)
 
     def to_neighbours(stage, sources, targets):
@@ -206,6 +209,15 @@
             ))
         return copies
 
+    for copy in loads:
+        copy.wait()
+    lists_ref[...] = jnp.zeros_like(lists_ref)
+    lists_ref[0:slots, 0:nblk] = own_lists[...]
+    list_copies = to_neighbours(0, [lists_ref, lists_ref], [near_lists.at[0], near_lists.at[1]])
+    for copy in list_copies:
+        copy.start()
+
+
     def gather(src, place, start, stop, sent, arrived):
         def send(i, carry):
             to = peer_of(i, me, tiles)
@@ -228,16 +240,17 @@
     qg_land = (lambda t: q_ref.at[t], lambda t: g_ref.at[t])
     local = []
     for a, src in enumerate((k_in, v_in)):
-        gather(src, kv_land[a], 1, tiles, send_sem.at[a], lambda i: recv_sem.at[a])
+        stage[a].wait()
+        gather(staged.at[a], kv_land[a], 1, tiles, send_sem.at[a], lambda i: recv_sem.at[a])
         local.append(keep_own(src, kv_land[a], local_sem.at[a]))
 
     def gather_qg(start, stop):
         def send(i, carry):
             i = near_first(i, tiles)
             to = peer_of(i, me, tiles)
-            for a, src in enumerate((q_in, g_in)):
+            for a in range(2):
                 pltpu.make_async_remote_copy(
-                    src_ref=src.at[:, pl.ds(pl.multiple_of(to * D, D), D)], dst_ref=qg_land[a](me),
+                    src_ref=staged.at[2 + a, :, pl.ds(pl.multiple_of(to * D, D), D)], dst_ref=qg_land[a](me),
                     send_sem=send_sem.at[2 + a], recv_sem=qg_sem.at[a, i],
                     device_id={"tile": to}, device_id_type=MESH,
                 ).start()
@@ -247,15 +260,8 @@
 
     for a, src in enumerate((q_in, g_in)):
         local.append(keep_own(src, qg_land[a], qg_sem.at[a, 0]))
-    gather_qg(1, tiles // 2)
-
-    for copy in loads:
-        copy.wait()
-    lists_ref[...] = jnp.zeros_like(lists_ref)
-    lists_ref[0:slots, 0:nblk] = own_lists[...]
-    list_copies = to_neighbours(0, [lists_ref, lists_ref], [near_lists.at[0], near_lists.at[1]])
-    for copy in list_copies:
-        copy.start()
+    stage[2].wait()
+    stage[3].wait()
 
     table[...] = jnp.zeros_like(table)
     table[COUNT : COUNT + 1, 0:nblk] = counts[...]
@@ -285,6 +291,8 @@
         )
         for copy in kv_copies[-2:]:
             copy.start()
+        if a == 0:
+            gather_qg(1, tiles // 2)
         keep.append(pltpu.make_async_copy(own[a], kv.at[pl.ds(0, nblk), :, cut], local_sem.at[4 + a]))
         keep[a].start()
     gather_qg(tiles // 2, tiles)
@@ -314,39 +322,34 @@
             [[scalars[PLACE, s * nblk + r] for s in range(slots)] for r in rs],
             slots, nblk, q_ref, g_ref, kv, kt, terms, dq_ref,
         )
+        for step, r in zip(steps, rs):
+            @pl.when(step > 0)
+            def _(r=r):
+                pltpu.make_async_remote_copy(
+                    src_ref=dq_ref.at[r], dst_ref=dq_out.at[:, mine],
+                    send_sem=send_sem.at[4], recv_sem=recv_sem.at[4],
+                    device_id={"tile": r}, device_id_type=MESH,
+                ).start()
         return carry
 
     lax.fori_loop(0, nblk // GROUP, blocks, 0)
-
-    def send_dq(i, carry):
-        to = peer_of(far_first(i, tiles), me, tiles)
-        pltpu.make_async_remote_copy(
-            src_ref=dq_ref.at[to], dst_ref=dq_out.at[:, mine],
-            send_sem=send_sem.at[4], recv_sem=recv_sem.at[4],
-            device_id={"tile": to}, device_id_type=MESH,
-        ).start()
-        return carry
-
-    lax.fori_loop(1, tiles, send_dq, 0)
     finals = [pltpu.make_async_copy(dq_ref.at[me], dq_out.at[:, mine], local_sem.at[0])]
     finals[0].start()
 
-    def add(i, total):
-        for u in range(STEPS):
-            t = i * STEPS + u
-            term = terms[scalars[PAIR, t]]
-            r = scalars[QUERY, t]
-            term = jnp.concatenate([f32dot(term[:, :D], q_ref[r]), f32dot(term[:, D:], g_ref[r])], 1)
-            total = jnp.where(scalars[SAME, t] > 0, total, 0.0) + term
-            sums[t] = total
-        return total
-
-    lax.fori_loop(0, pairs // STEPS, add, jnp.zeros((D, 2 * D), jnp.float32))
-
     parts = (parts_k, parts_v)
     part_copies = []
-    for a in (1, 0):
+    for a, rows in ((1, g_ref), (0, q_ref)):
         cut = pl.ds(a * D, D)
+
+        def add(i, total, rows=rows, cut=cut):
+            for u in range(STEPS):
+                t = i * STEPS + u
+                term = f32dot(terms[scalars[PAIR, t], :, cut], rows[scalars[QUERY, t]])
+                total = jnp.where(scalars[SAME, t] > 0, total, 0.0) + term
+                sums[t, :, cut] = total
+            return total
+
+        lax.fori_loop(0, pairs // STEPS, add, jnp.zeros((D, D), jnp.float32))
         for side in range(2):
             def part(n, carry, a=a, side=side, cut=cut):
                 j = nblk + side * NEAR + n
@@ -400,13 +403,19 @@
         wait_bytes(q_ref.at[pl.ds(0, tiles - 1)], recv_sem.at[a])
 
 
-def hand_over(a_in, b_in, c_in, a_out, b_out, c_out, sem):
-    copies = []
+def hand_over(a_in, b_in, c_in, a_out, b_out, c_out, held, in_sem, out_sem):
+    loads, stores = [], []
     for i, (src, dst) in enumerate(((a_in, a_out), (b_in, b_out), (c_in, c_out))):
-        copies.append(pltpu.make_async_copy(src, dst, sem.at[i]))
-        copies[-1].start()
-    for copy in copies:
-        copy.wait()
+        for j in range(2):
+            rows = pl.ds(j * (D // 2), D // 2)
+            loads.append(pltpu.make_async_copy(src.at[rows], held.at[i, rows], in_sem.at[i, j]))
+            stores.append(pltpu.make_async_copy(held.at[i, rows], dst.at[rows], out_sem.at[i, j]))
+            loads[-1].start()
+    for load, store in zip(loads, stores):
+        load.wait()
+        store.start()
+    for store in stores:
+        store.wait()
 
 
 def local(tiles, frames, queries, keys, values, out_grad, key_lists, key_counts):
@@ -437,9 +446,11 @@
             pltpu.VMEM((2, 8, 128), i32),
             pltpu.VMEM((16, 256), i32),
             pltpu.SMEM((16, 256), i32),
+            pltpu.VMEM((4, D, tiles * D), bf16),
             pltpu.SemaphoreType.DMA((7,)),
             pltpu.SemaphoreType.DMA((7,)),
             pltpu.SemaphoreType.DMA((2, nblk)),
+            pltpu.SemaphoreType.DMA((4,)),
             pltpu.SemaphoreType.DMA((6,)),
             pltpu.SemaphoreType.DMA((5, 2)),
             pltpu.SemaphoreType.DMA((5, 2)),
@@ -452,9 +463,14 @@
     return pl.pallas_call(
         hand_over,
         out_shape=(out, out, out),
-        in_specs=[VMEM] * 3,
+        in_specs=[ANY] * 3,
         out_specs=(ANY, ANY, ANY),
-        scratch_shapes=[pltpu.SemaphoreType.DMA((3,))],
+        scratch_shapes=[
+            pltpu.VMEM((3, D, tiles * D), bf16),
+            pltpu.SemaphoreType.DMA((3, 2)),
+            pltpu.SemaphoreType.DMA((3, 2)),
+        ],
+        compiler_params=pltpu.CompilerParams(vmem_limit_bytes=60 * 2**20),
         name="hand_over",
     )(*grads)
 

time: 150 us -> 143 us (0.953); the launches traced: 150 us -> 141 us
  Pallas kernels: 149 us -> 141 us
    pallas_call x1, Pallas kernels: 146 us -> 138 us  [local(): pl.pallas_call(functools.partial(kernel, tiles, frames, slots), out_shape...]
where the time goes in v4:
time: 143 us; the launch traced here: 141 us
  Pallas kernels  141 us (99%)
    pallas_call x1, Pallas kernels, local(): pl.pallas_call(functools.partial(kernel, tiles, frames, slots), out_shape...  138 us

profile of v4, /device:TPU:1, one launch (start us, length us, event | category | flops | bytes accessed | tf_op | source)
XLA Modules:
  0.0 141.5 jit_solution(4625303919351459456)
XLA Ops:
  0.6 138.0 %backward.1 = (bf16[128,4096]{1,0:T(8,128)(2,1)}, bf16[128,4096]{1,0:T(8,128)(2,1)}, bf16[128,4096]{1,0:T(8,128)(2,1)}) custom-call(s32[6,32]{1,0:T(8,128)} %bitcast.2, s32[1,32]{1,0:T(1,128)} %bitcast.3, bf16[128,4096]{1,0:T(8,128)(2,1)} %q_in.1, bf16[128,4096]{1,0:T(8,128)(2,1)} %k_in.1, bf16[128,4096]{1,0:T(8,128)(2,1)} %v_in.1, bf16[128,4096]{1,0:T(8,128)(2,1)} %g_in.1), custom_call_target="tpu_custom_call" | custom-call | tf_op jit(solution)/shard_map/backward/pallas_call | solution.py:425
  138.7 2.8 %hand_over.1 = (bf16[128,4096]{1,0:T(8,128)(2,1)}, bf16[128,4096]{1,0:T(8,128)(2,1)}, bf16[128,4096]{1,0:T(8,128)(2,1)}) custom-call(bf16[128,4096]{1,0:T(8,128)(2,1)} %get-tuple-element.6.a_in, bf16[128,4096]{1,0:T(8,128)(2,1)} %get-tuple-element.7.b_in, bf16[128,4096]{1,0:T(8,128)(2,1)} %get-tuple-element.8.c_in), custom_call_target="tpu_custom_call" | custom-call | tf_op jit(solution)/shard_map/hand_over/pallas_call | solution.py:463

commit v5 on v4

--- a/solution.py
+++ b/solution.py
@@ -14,7 +14,7 @@
 SCALE = D ** (-0.5)
 LOG2E = 1.4426950408889634
 GROUP = 4
-STEPS = 16
+STEPS = 32
 PLACE, PAIR, QUERY, SAME, LAST, HAS, COUNT, NAMED, RANK, PICK = 0, 1, 2, 3, 4, 5, 6, 7, 9, 11
 
 

time: 143 us -> 142 us (level); the launches traced: 141 us -> 142 us
  no operation moved by 1% of the time
where the time goes in v5:
time: 142 us
  Pallas kernels  141 us (99%)
    pallas_call x1, Pallas kernels, local(): pl.pallas_call(functools.partial(kernel, tiles, frames, slots), out_shape...  139 us

profile of v5, /device:TPU:1, one launch (start us, length us, event | category | flops | bytes accessed | tf_op | source)
XLA Modules:
  0.0 142.0 jit_solution(13014495124126359398)
XLA Ops:
  0.6 138.5 %backward.1 = (bf16[128,4096]{1,0:T(8,128)(2,1)}, bf16[128,4096]{1,0:T(8,128)(2,1)}, bf16[128,4096]{1,0:T(8,128)(2,1)}) custom-call(s32[6,32]{1,0:T(8,128)} %bitcast.2, s32[1,32]{1,0:T(1,128)} %bitcast.3, bf16[128,4096]{1,0:T(8,128)(2,1)} %q_in.1, bf16[128,4096]{1,0:T(8,128)(2,1)} %k_in.1, bf16[128,4096]{1,0:T(8,128)(2,1)} %v_in.1, bf16[128,4096]{1,0:T(8,128)(2,1)} %g_in.1), custom_call_target="tpu_custom_call" | custom-call | tf_op jit(solution)/shard_map/backward/pallas_call | solution.py:425
  139.2 2.8 %hand_over.1 = (bf16[128,4096]{1,0:T(8,128)(2,1)}, bf16[128,4096]{1,0:T(8,128)(2,1)}, bf16[128,4096]{1,0:T(8,128)(2,1)}) custom-call(bf16[128,4096]{1,0:T(8,128)(2,1)} %get-tuple-element.6.a_in, bf16[128,4096]{1,0:T(8,128)(2,1)} %get-tuple-element.7.b_in, bf16[128,4096]{1,0:T(8,128)(2,1)} %get-tuple-element.8.c_in), custom_call_target="tpu_custom_call" | custom-call | tf_op jit(solution)/shard_map/hand_over/pallas_call | solution.py:463
